TPU v7x, 256 devices: a whole 4x4x8 slice. The times are simulated.
256 devices in a mesh: wide: 64 (over y, z, x_hi), narrow: 4 (over x_lo, core).
Axes of the slice: x: 4 (x_hi: 2, x_lo: 2; x = x_hi * 2 + x_lo), y: 4, z: 8, core: 2. Of those that a mesh axis runs over, the one named last changes fastest.
Arguments:
- volume: bfloat16 [128, 64, 64, 128], P('wide', 'narrow'), may hold values from -16 to 16
- down_weight: bfloat16 [1024, 256], replicated, may hold values from -0.1875 to 0.1875
- conv_weight: bfloat16 [27, 256, 256], replicated, may hold values from -0.078125 to 0.078125
- cotangent: bfloat16 [64, 32, 32, 256], P('wide', None, None, 'narrow'), may hold values from -16 to 16
Outputs:
- activated: bfloat16 [64, 32, 32, 256], P('wide', None, None, 'narrow')
- volume_grad: bfloat16 [128, 64, 64, 128], P('wide', 'narrow')
- down_grad: float32 [1024, 256], P(('wide', 'narrow'))
- conv_grad: float32 [27, 256, 256], P(None, 'narrow', 'wide')
All inputs are finite; a program needn't handle non-finite values.
Results may differ from a plain program's by a relative error of at most 0.0095.
Values may be sent and summed in bfloat16 or wider, within the bound.
A program may use at most 64 MiB of HBM per device.

v0:
```python
import math

import jax
import jax.numpy as jnp
from jax import lax
from jax.sharding import PartitionSpec as P


def extended(block, sides, width):
    for axis, dim in sides:
        count = lax.axis_size(axis)
        forward = [(i, i + 1) for i in range(count - 1)]
        backward = [(target, source) for source, target in forward]
        low = lax.ppermute(
            lax.slice_in_dim(block, block.shape[dim] - width, None, axis=dim), axis, forward
        )
        high = lax.ppermute(lax.slice_in_dim(block, 0, width, axis=dim), axis, backward)
        block = jnp.concatenate([low, block, high], axis=dim)
    return block


def tap_offsets(t):
    return (t // 9, t // 3 % 3, t % 3)


def silu_slope(values):
    sigma = jax.nn.sigmoid(values)
    return sigma * (1.0 + values * (1.0 - sigma))


def pad_sides(field, dims):
    widths = [(1, 1) if d in dims else (0, 0) for d in range(4)]
    return jnp.pad(field, widths)


def conv_forward(padded, weights, planes, rows, cols):
    channels = padded.shape[3]
    total = jnp.zeros((planes * rows * cols, weights.shape[2]), jnp.float32)
    for t in range(27):
        i, j, k = tap_offsets(t)
        slab = padded[i : i + planes, j : j + rows, k : k + cols].reshape(-1, channels)
        total = total + jnp.dot(slab, weights[t], preferred_element_type=jnp.float32)
    return total


def conv_backward(grad_padded, input_padded, weights, center, planes, rows, cols):
    width_out = grad_padded.shape[3]
    width_in = input_padded.shape[3]
    grad_input = jnp.zeros((planes * rows * cols, weights.shape[1]), jnp.float32)
    weight_terms = []
    for t in range(27):
        i, j, k = tap_offsets(t)
        grad_slab = grad_padded[
            2 - i : 2 - i + planes, 2 - j : 2 - j + rows, 2 - k : 2 - k + cols
        ].reshape(-1, width_out)
        grad_input = grad_input + lax.dot_general(
            grad_slab, weights[t], (((1,), (1,)), ((), ())), preferred_element_type=jnp.float32
        )
        slab = input_padded[i : i + planes, j : j + rows, k : k + cols].reshape(-1, width_in)
        weight_terms.append(
            lax.dot_general(
                slab, center, (((0,), (0,)), ((), ())), preferred_element_type=jnp.float32
            )
        )
    return (grad_input, jnp.stack(weight_terms))


def on_device(volume, down_weight, conv_weight, cotangent):
    planes = volume.shape[0] // 2
    rows = volume.shape[1] // 2
    cols = volume.shape[2] // 2
    chan_in = volume.shape[3]
    chan_out = down_weight.shape[1]
    narrow_count = lax.axis_size("narrow")
    quarter = chan_out // narrow_count
    side_cells = rows * narrow_count
    depth_total = planes * lax.axis_size("wide")
    factor = 1.0 / (side_cells * math.sqrt(depth_total))
    patches = volume.reshape(planes, 2, rows, 2, cols, 2, chan_in)
    patches = patches.transpose(0, 2, 4, 1, 3, 5, 6).reshape(planes * rows * cols, 8 * chan_in)
    deep = jnp.dot(patches, down_weight, preferred_element_type=jnp.float32).astype(jnp.bfloat16)
    deep = deep.reshape(planes, rows, cols, chan_out)
    group = lax.axis_index("narrow")
    deep_group = lax.all_to_all(deep, "narrow", split_axis=3, concat_axis=1, tiled=True)
    deep_rims = extended(deep_group, (("wide", 0),), 1)
    own_padded = pad_sides(deep_rims, (1, 2))
    weight_out = lax.dynamic_slice_in_dim(conv_weight, group * quarter, quarter, 2)
    weight_in = lax.dynamic_slice_in_dim(conv_weight, group * quarter, quarter, 1)
    piece = lax.all_gather(deep_rims, "narrow", axis=3, tiled=True)
    weights = weight_out
    preact = conv_forward(pad_sides(piece, (1, 2)), weights, planes, side_cells, cols)
    activated = jax.nn.silu(preact).astype(jnp.bfloat16).reshape(planes, side_cells, cols, quarter)
    grad_pre = cotangent.astype(jnp.float32).reshape(-1, quarter) * silu_slope(preact)
    grad_pre = grad_pre.astype(jnp.bfloat16).reshape(planes, side_cells, cols, quarter)
    grad_rims = extended(grad_pre, (("wide", 0),), 1)
    piece = lax.all_gather(grad_rims, "narrow", axis=3, tiled=True)
    width = piece.shape[3]
    weights = weight_in
    center = piece[1 : 1 + planes].reshape(-1, width)
    grad_term, weight_term = conv_backward(
        pad_sides(piece, (1, 2)), own_padded, weights, center, planes, side_cells, cols
    )
    grad_group = grad_term.astype(jnp.bfloat16).reshape(planes, side_cells, cols, quarter)
    grad_deep = lax.all_to_all(grad_group, "narrow", split_axis=1, concat_axis=3, tiled=True)
    conv_grad = lax.psum_scatter(weight_term * factor, "wide", scatter_dimension=2, tiled=True)
    grad_flat = grad_deep.reshape(planes * rows * cols, chan_out)
    down_grad = lax.psum_scatter(
        lax.dot_general(
            patches, grad_flat, (((0,), (0,)), ((), ())), preferred_element_type=jnp.float32
        )
        * factor,
        ("wide", "narrow"),
        scatter_dimension=0,
        tiled=True,
    )
    volume_grad = lax.dot_general(
        grad_flat, down_weight, (((1,), (1,)), ((), ())), preferred_element_type=jnp.float32
    ).astype(jnp.bfloat16)
    volume_grad = volume_grad.reshape(planes, rows, cols, 2, 2, 2, chan_in)
    volume_grad = volume_grad.transpose(0, 3, 1, 4, 2, 5, 6).reshape(
        2 * planes, 2 * rows, 2 * cols, chan_in
    )
    return (activated, volume_grad, down_grad, conv_grad)


def solution(mesh):
    placed = (P("wide", "narrow", None, None), P(), P(), P("wide", None, None, "narrow"))
    return jax.shard_map(
        on_device,
        mesh=mesh,
        in_specs=placed,
        out_specs=(
            P("wide", None, None, "narrow"),
            P("wide", "narrow", None, None),
            P(("wide", "narrow"), None),
            P(None, "narrow", "wide"),
        ),
        check_vma=False,
    )
```

profile of v0, /device:TPU:2, one launch (start us, length us, event | category | flops | bytes accessed | tf_op | source)
XLA Modules:
  0.0 929.5 jit_solution(2517090128293368973)
XLA Ops:
  7.2 2.3 copy.70
  18.1 9.2 all_to_all.33
  31.4 2.6 collective-permute-start
  35.3 10.3 %collective-permute-done = bf16[1,32,32,64]{3,2,1,0:T(8,128)(2,1)S(1)} collective-permute-done((bf16[1,32,32,64]{3,2,1,0:T(8,128)(2,1)}, bf16[1,32,32,64]{3,2,1,0:T(8,128)(2,1)S(1)}, u32[]{:S(2)}, u32[]{:S(2)}) %collective-permute-start) | collective-permute-done | bytes 131104 | tf_op jit(solution)/shard_map/ppermute | solution.py:14
  45.6 5.5 collective-permute-done.1
  53.9 3.1 copy.46
  60.7 61.5 %all-gather.3.cloned.1.call-done = bf16[3,32,32,256]{2,1,0,3:T(8,128)(2,1)} async-done(((bf16[3,32,32,64]{2,1,0,3:T(8,128)(2,1)}), bf16[3,32,32,256]{2,1,0,3:T(8,128)(2,1)}) %all-gather.3.cloned.1.call-update) | async-done | bytes 1572880 | tf_op jit(solution)/shard_map/all_gather | solution.py:89
  122.2 7.8 copy.47
  130.0 3.6 pad_slice_fusion.25
  133.7 4.2 pad_slice_fusion.24
  150.2 4.2 collective-permute-start.2
  155.9 10.8 %collective-permute-done.2 = bf16[1,32,32,64]{3,2,1,0:T(8,128)(2,1)S(1)} collective-permute-done((bf16[1,32,32,64]{3,2,1,0:T(8,128)(2,1)}, bf16[1,32,32,64]{3,2,1,0:T(8,128)(2,1)S(1)}, u32[]{:S(2)}, u32[]{:S(2)}) %collective-permute-start.2) | collective-permute-done | bytes 131104 | tf_op jit(solution)/shard_map/ppermute | solution.py:14
  166.7 4.9 collective-permute-done.3
  173.6 3.0 copy.54
  176.7 63.8 %all-gather.5.cloned.1.call-done = bf16[3,32,32,256]{2,1,0,3:T(8,128)(2,1)} async-done(((bf16[3,32,32,64]{2,1,0,3:T(8,128)(2,1)}), bf16[3,32,32,256]{2,1,0,3:T(8,128)(2,1)}) %all-gather.5.cloned.1.call-update) | async-done | bytes 1572880 | tf_op jit(solution)/shard_map/all_gather | solution.py:96
  240.5 7.8 copy.55
  249.8 6.5 pad_slice_fusion
  276.3 5.3 all-to-all-start.1
  290.0 2.4 fusion
  294.6 2.9 broadcast_multiply_fusion
  297.5 5.5 copy.63
  309.2 2.4 copy.62
  311.6 239.2 %all-reduce.6.cloned.1.call-done = f32[1024,256]{0,1:T(8,128)} async-done(((f32[1024,256]{0,1:T(8,128)}), f32[1024,256]{0,1:T(8,128)}) %all-reduce.6.cloned.1.call-update) | async-done | bytes 1048592
  554.0 367.4 %reduce-scatter.3.cloned.1.call-done = f32[27,64,4]{1,0,2:T(8,128)} async-done(((f32[27,64,256]{1,0,2:T(8,128)}), f32[27,64,4]{1,0,2:T(8,128)}) %reduce-scatter.3.cloned.1.call-update) | async-done | bytes 27664 | tf_op jit(solution)/shard_map/reduce_scatter | solution.py:105
  (137 shorter events, 78.9 us)
Async XLA Ops:
  7.2 130.7 %copy-start = (bf16[27,256,256]{2,1,0:T(8,128)(2,1)S(1)}, bf16[27,256,256]{2,1,0:T(8,128)(2,1)}, u32[]{:S(2)}) copy-start(bf16[27,256,256]{2,1,0:T(8,128)(2,1)} %param.6) | copy-start | bytes 10616836
  7.2 115.0 %all-gather.3.cloned.1.call-start = ((), (), s32[]{:S(2)}) async-start(), calls=%async_computation.3 | async-start | bytes 7864320 | tf_op jit(solution)/shard_map/all_gather | solution.py:89
  31.4 14.2 %collective-permute-start = (bf16[1,32,32,64]{3,2,1,0:T(8,128)(2,1)}, bf16[1,32,32,64]{3,2,1,0:T(8,128)(2,1)S(1)}, u32[]{:S(2)}, u32[]{:S(2)}) collective-permute-start(bf16[1,32,32,64]{3,2,1,0:T(8,128)(2,1)} %bitcast.580), channel_id=1, source_target_pairs={{0,4},{4,8},{8,12},{12,16},{16,20},{20,24},{24,28},{28,32},{32,36}... | collective-permute-start | bytes 393224 | tf_op jit(solution)/shard_map/ppermute | solution.py:14
  34.0 17.1 %collective-permute-start.1 = (bf16[1,32,32,64]{3,2,1,0:T(8,128)(2,1)}, bf16[1,32,32,64]{3,2,1,0:T(8,128)(2,1)S(1)}, u32[]{:S(2)}, u32[]{:S(2)}) collective-permute-start(bf16[1,32,32,64]{3,2,1,0:T(8,128)(2,1)} %bitcast.581), channel_id=1, source_target_pairs={{4,0},{8,4},{12,8},{16,12},{20,16},{24,20},{28,24},{32,28},{36,32}... | collective-permute-start | bytes 393224 | tf_op jit(solution)/shard_map/ppermute | solution.py:17
  45.6 5.5 copy-start.8
  51.1 0.7 copy-start.6
  57.0 183.6 %all-gather.5.cloned.1.call-start = ((), (), s32[]{:S(2)}) async-start(), calls=%async_computation.4 | async-start | bytes 7864320 | tf_op jit(solution)/shard_map/all_gather | solution.py:96
  130.0 3.7 copy-start.3
  145.9 1.5 copy-start.10
  150.2 16.5 %collective-permute-start.2 = (bf16[1,32,32,64]{3,2,1,0:T(8,128)(2,1)}, bf16[1,32,32,64]{3,2,1,0:T(8,128)(2,1)S(1)}, u32[]{:S(2)}, u32[]{:S(2)}) collective-permute-start(bf16[1,32,32,64]{3,2,1,0:T(8,128)(2,1)} %bitcast.644), channel_id=1, source_target_pairs={{0,4},{4,8},{8,12},{12,16},{16,20},{20,24},{24,28},{28,32},{32,36}... | collective-permute-start | bytes 393224 | tf_op jit(solution)/shard_map/ppermute | solution.py:14
  154.4 17.2 %collective-permute-start.3 = (bf16[1,32,32,64]{3,2,1,0:T(8,128)(2,1)}, bf16[1,32,32,64]{3,2,1,0:T(8,128)(2,1)S(1)}, u32[]{:S(2)}, u32[]{:S(2)}) collective-permute-start(bf16[1,32,32,64]{3,2,1,0:T(8,128)(2,1)} %bitcast.645), channel_id=1, source_target_pairs={{4,0},{8,4},{12,8},{16,12},{20,16},{24,20},{28,24},{32,28},{36,32}... | collective-permute-start | bytes 393224 | tf_op jit(solution)/shard_map/ppermute | solution.py:17
  249.8 6.6 copy-start.2
  256.3 1.1 copy-start.1
  257.5 0.9 copy-start.9
  260.0 1.0 copy-start.4
  262.5 1.0 copy-start.7
  264.3 1.4 copy-start.5
  276.3 8.2 all-to-all-start.1
  281.6 269.2 %all-reduce.6.cloned.1.call-start = ((), (), s32[]{:S(2)}) async-start(), calls=%async_computation.6 | async-start | bytes 2097152
  292.5 629.0 %reduce-scatter.3.cloned.1.call-start = ((), (), s32[]{:S(2)}) async-start(), calls=%async_computation.5 | async-start | bytes 4259840 | tf_op jit(solution)/shard_map/reduce_scatter | solution.py:105
Sparse Core Ops, SparseCore 0:
  57.1 65.0 all-gather.2
  176.8 63.6 all-gather.4
  292.6 258.1 all-reduce.5
  553.3 368.0 reduce-scatter.2
where the time goes:
time: 931 us; the launch traced here: 929 us
  waiting for transfers between devices  764 us (82%)
  local copies, waits for them, and re-layouts  80.6 us (9%)
  matrix products  37.4 us (4%)
  starting transfers between devices  15 us (2%)
  between operations  14.2 us (2%)
    reduce_scatter x1, waiting for transfers between devices, on_device(): lax.psum_scatter(weight_term * factor, 'wide', scatter_dimension=2, tiled...  367 us
    unnamed x5, waiting for transfers between devices  239 us
    all_gather x1, waiting for transfers between devices, on_device(): piece = lax.all_gather(grad_rims, 'narrow', axis=3, tiled=True)  63.8 us
    all_gather x1, waiting for transfers between devices, on_device(): piece = lax.all_gather(deep_rims, 'narrow', axis=3, tiled=True)  61.5 us
    ppermute x2, waiting for transfers between devices, extended(): lax.ppermute(lax.slice_in_dim(block, block.shape[dim] - width, None, axis...  21.1 us
  transfers between devices with their start and end apart: 9, of which 9 were waited for; matrix products, arithmetic and copies ran while one was open for 3% of the time, Pallas kernels for 0%

commit v1 on v0

v1 whole, which is shorter than its diff:
```python
import functools
import math

import jax
import jax.numpy as jnp
from jax import lax
from jax.experimental import pallas as pl
from jax.experimental.pallas import tpu as pltpu
from jax.sharding import PartitionSpec as P

MESH = pl.DeviceIdType.MESH
BF = jnp.bfloat16
F32 = jnp.float32
NY, NZ = 4, 8

COT = 0
DEEP_HALO = 3
DEEP_SHARE = 11
ACT = 20
GRAD_HALO = 23
GRAD_SHARE = 31
CONV_Y = 34
CONV_Z = 43
DOWN_N = 64
DOWN_Y = 67
DOWN_Z = 70
LAST = 77
MESSAGES = 80


def matmul(a, b):
    return jnp.dot(a, b, preferred_element_type=F32)


def matmul_nt(a, b):
    return lax.dot_general(a, b, (((1,), (1,)), ((), ())), preferred_element_type=F32)


def kernel(
    factor,
    vol_ref,
    dw_ref,
    cw_ref,
    cot_ref,
    act_out,
    vg_out,
    dg_out,
    cg_out,
    vol,
    dw,
    cw,
    cot,
    wide_f32,
    patches,
    patches_t,
    deep,
    grad,
    deep_all,
    grad_t_send,
    grad_t,
    grad_rows,
    acc,
    cot_send,
    cot_recv,
    act_send,
    act_recv,
    cy_send,
    cy_recv,
    sum_rows,
    z_rows,
    cz_send,
    cz_recv,
    dn_rows,
    dn_send,
    dn_recv,
    dy_send,
    dy_recv,
    dz_send,
    dz_recv,
    last_send,
    last_recv,
    local_sem,
    send_sem,
    recv_sem,
):
    w = lax.axis_index("wide")
    n = lax.axis_index("narrow")
    y, z, xh = w // 16, (w // 2) % NZ, w % 2
    l, c = n // 2, n % 2

    def wide_of(yy, zz, xx):
        return ((yy % NY) * NZ + zz % NZ) * 2 + xx

    near = [(w, (n + d) % 4) for d in range(1, 4)]
    up, down = (w + 1) % 64, (w + 63) % 64
    right, left = (n + 1) % 4, (n + 3) % 4
    depth = [(s, m) for s in (up, down) for m in (n, right, left)]
    ys = [(wide_of(y + d, z, xh), n) for d in range(1, NY)]
    zs = [(wide_of(y, z + d, xh), n) for d in range(1, NZ)]
    other_c = n + 1 - 2 * c
    lasts = [(wide_of(y, z, 1 - xh), n), (wide_of(y, z, 1 - xh), other_c), (w, other_c)]

    barrier = pltpu.get_barrier_semaphore()
    partners = near + depth + ys + zs + lasts[:2]
    for who in partners:
        pl.semaphore_signal(barrier, inc=1, device_id=who, device_id_type=MESH)

    started = []

    def send(number, src, dst, who):
        copy = pltpu.make_async_remote_copy(
            src_ref=src,
            dst_ref=dst,
            send_sem=send_sem.at[number],
            recv_sem=recv_sem.at[number],
            device_id=who,
            device_id_type=MESH,
        )
        copy.start()
        started.append(copy)
        return copy

    loads = [
        pltpu.make_async_copy(src, dst, local_sem.at[s])
        for s, (src, dst) in enumerate(((cot_ref, cot), (vol_ref, vol), (dw_ref, dw), (cw_ref, cw)))
    ]
    for copy in loads:
        copy.start()

    deep_all[:, 0:1] = jnp.zeros((3, 1, 32, 128), BF)
    deep_all[:, 33:34] = jnp.zeros((3, 1, 32, 128), BF)
    z_rows[...] = jnp.zeros_like(z_rows)

    loads[0].wait()
    for m in range(4):
        cot_send[m] = jnp.concatenate([cot[m, :128], cot[m, 128:]], axis=1)
    cot_recv[pl.ds(n, 1)] = cot_send[pl.ds(n, 1)]
    pl.semaphore_wait(barrier, len(partners))
    cot_copies = [
        send(COT + d - 1, cot_send.at[(n + d) % 4], cot_recv.at[n], near[d - 1]) for d in range(1, 4)
    ]

    loads[1].wait()
    wide_f32[...] = vol[...].astype(F32)
    for a in range(2):
        for b in range(2):
            for e in range(2):
                part = wide_f32[a, :, b, pl.ds(e, 32, stride=2), :].reshape(256, 128).astype(BF)
                at = (4 * a + 2 * b + e) * 128
                patches[:, at : at + 128] = part
    loads[2].wait()
    cells = matmul(patches[...], dw[...]).astype(BF)
    for half in range(2):
        deep[half, 1, 1:9] = cells[:, 128 * half : 128 * half + 128].reshape(8, 32, 128)

    def send_halos(buf, base):
        copies = []
        for s, (to, plane) in enumerate(((up, 0), (down, 2))):
            copies.append(
                send(base + s, buf.at[:, 1, pl.ds(1, 8)], buf.at[:, plane, pl.ds(1, 8)], (to, n))
            )
        for s, (to, plane) in enumerate(((w, 1), (up, 0), (down, 2))):
            copies.append(
                send(base + 2 + 2 * s, buf.at[:, 1, pl.ds(8, 1)], buf.at[:, plane, pl.ds(0, 1)], (to, right))
            )
            copies.append(
                send(base + 3 + 2 * s, buf.at[:, 1, pl.ds(1, 1)], buf.at[:, plane, pl.ds(9, 1)], (to, left))
            )
        return copies

    def rows_arrive(buf, copies, plane):
        s = {1: 0, 0: 1, 2: 2}[plane]
        copies[2 + 2 * s].wait_recv()
        copies[3 + 2 * s].wait_recv()

        @pl.when(n == 0)
        def _():
            buf[:, plane, 0:1] = jnp.zeros((2, 1, 32, 128), BF)

        @pl.when(n == 3)
        def _():
            buf[:, plane, 9:10] = jnp.zeros((2, 1, 32, 128), BF)

    def plane_arrives(buf, copies, plane):
        copies[0 if plane == 0 else 1].wait_recv()
        rows_arrive(buf, copies, plane)

        @pl.when(w == (0 if plane == 0 else 63))
        def _():
            buf[:, plane] = jnp.zeros((2, 10, 32, 128), BF)

    def share_deep(plane):
        deep_all[plane, pl.ds(1 + 8 * n, 8)] = deep[pl.ds(l, 1), plane, 1:9].reshape(8, 32, 128)
        return [
            send(
                DEEP_SHARE + 3 * plane + d - 1,
                deep.at[((n + d) % 4) // 2, plane, pl.ds(1, 8)],
                deep_all.at[plane, pl.ds(1 + 8 * n, 8)],
                near[d - 1],
            )
            for d in range(1, 4)
        ]

    deep_halos = send_halos(deep, DEEP_HALO)
    shared = {1: share_deep(1)}
    for s in range(4):
        block = patches[:, 256 * s : 256 * s + 256].astype(F32)
        patches_t[256 * s : 256 * s + 256, :] = block.T.astype(BF)

    def window(buf, plane, first):
        return [buf[half, plane, first : first + 8].reshape(256, 128) for half in range(2)]

    def shifted(value, by, masked):
        column = lax.broadcasted_iota(jnp.int32, value.shape, 0) % 32
        return jnp.where(column == masked, 0.0, pltpu.roll(value, by, 0))

    loads[3].wait()
    for i in (1, 0, 2):
        if i == 1:
            rows_arrive(deep, deep_halos, 1)
        else:
            plane_arrives(deep, deep_halos, i)
            shared[i] = share_deep(i)
        slab = jnp.concatenate(window(deep, i, 0) + window(deep, i, 1) + window(deep, i, 2), axis=1)
        for k in range(3):
            weights = jnp.concatenate([cw[9 * i + 3 * j + k] for j in range(3)], axis=0)
            term = matmul(slab, weights)
            acc[k] = term if i == 1 else acc[k] + term
    preact = shifted(acc[0], 1, 0) + acc[1] + shifted(acc[2], 255, 31)

    for copy in cot_copies:
        copy.wait_recv()
    cotangent = jnp.concatenate(
        [
            jnp.concatenate([cot_recv[m][:, :64], cot_recv[m][:, 64:]], axis=0)
            for m in range(4)
        ],
        axis=1,
    ).astype(F32)
    sigma = 1.0 / (1.0 + jnp.exp(-preact))
    activated = (preact * sigma).astype(BF)
    grad_pre = (cotangent * (sigma * (1.0 + preact * (1.0 - sigma)))).astype(BF)
    for half in range(2):
        grad[half, 1, 1:9] = grad_pre[:, 128 * half : 128 * half + 128].reshape(8, 32, 128)

    row = lax.broadcasted_iota(jnp.int32, (256, 256), 0)
    column = lax.broadcasted_iota(jnp.int32, (256, 256), 1)
    q = row % 128
    source = (q // 32) * 64 + ((q // 4) % 8) * 8 + (row // 128) * 4 + q % 4
    order = jnp.where(column == source, 1.0, 0.0).astype(BF)
    turned = matmul_nt(order, grad_pre).astype(BF)
    grad_t_send[0] = turned[:128]
    grad_t_send[1] = turned[128:]
    grad_t[pl.ds(n, 1)] = grad_t_send[pl.ds(c, 1)]
    grad_shared = [
        send(GRAD_SHARE + d - 1, grad_t_send.at[(n + d) % 2], grad_t.at[n], near[d - 1])
        for d in range(1, 4)
    ]
    grad_halos = send_halos(grad, GRAD_HALO)

    for m in range(4):
        part = activated[:, 64 * m : 64 * m + 64]
        act_send[m] = jnp.concatenate([part[:128], part[128:]], axis=1)
    act_recv[pl.ds(n, 1)] = act_send[pl.ds(n, 1)]
    act_copies = [
        send(ACT + d - 1, act_send.at[(n + d) % 4], act_recv.at[n], near[d - 1]) for d in range(1, 4)
    ]

    for copy in grad_shared:
        copy.wait_recv()
    lane = lax.broadcasted_iota(jnp.int32, (128, 256), 1) % 32
    for m in range(4):
        block = grad_t[m].astype(F32)
        at = 256 * m
        grad_rows[0:128, at : at + 256] = jnp.where(lane == 31, 0.0, pltpu.roll(block, 255, 1)).astype(BF)
        grad_rows[128:256, at : at + 256] = grad_t[m]
        grad_rows[256:384, at : at + 256] = jnp.where(lane == 0, 0.0, pltpu.roll(block, 1, 1)).astype(BF)
    conv_y = {}
    for i in (1, 0, 2):
        for copy in shared[i]:
            copy.wait_recv()
        slab = jnp.concatenate([deep_all[i, j : j + 32].reshape(1024, 128) for j in range(3)], axis=1)
        term = matmul(grad_rows[...], slab).astype(BF)
        for yy in range(NY):
            for k in range(3):
                at = 128 * k + 32 * yy
                cy_send[i, yy, k] = term[at : at + 32]
        conv_y[i] = [
            send(CONV_Y + 3 * i + d - 1, cy_send.at[i, (y + d) % NY], cy_recv.at[i, d - 1], ys[d - 1])
            for d in range(1, NY)
        ]

    for i in (1, 2, 0):
        plane = 2 - i
        if i == 1:
            rows_arrive(grad, grad_halos, 1)
        else:
            plane_arrives(grad, grad_halos, plane)
        slab = jnp.concatenate(
            window(grad, plane, 2) + window(grad, plane, 1) + window(grad, plane, 0), axis=1
        )
        for k in range(3):
            weights = jnp.concatenate([cw[9 * i + 3 * j + k] for j in range(3)], axis=1)
            term = matmul_nt(slab, weights)
            acc[k] = term if i == 1 else acc[k] + term
    grad_deep = (shifted(acc[0], 255, 31) + acc[1] + shifted(acc[2], 1, 0)).astype(BF)

    partial = matmul(patches_t[...], grad_deep).reshape(32, 2, 2, 8, 256)
    for ll in range(2):
        for cc in range(2):
            for xx in range(2):
                dn_rows[ll, cc, :, 8 * xx : 8 * xx + 8] = partial[:, xx, ll, :, 128 * cc : 128 * cc + 128]
    dn_send[...] = dn_rows[...].astype(BF)
    down_n = [
        send(
            DOWN_N + d - 1,
            dn_send.at[((n + d) % 4) // 2, (n + d) % 2],
            dn_recv.at[d - 1],
            near[d - 1],
        )
        for d in range(1, 4)
    ]

    spread = matmul_nt(grad_deep, dw[...])
    for a in range(2):
        for b in range(2):
            for e in range(2):
                at = (4 * a + 2 * b + e) * 128
                wide_f32[a, :, b, pl.ds(e, 32, stride=2), :] = spread[:, at : at + 128].reshape(8, 32, 128)
    vg_out[...] = wide_f32[...].astype(BF)

    def conv_after_y(i):
        for copy in conv_y[i]:
            copy.wait_recv()
        total = cy_send[pl.ds(i, 1), pl.ds(y, 1)].reshape(3, 32, 384).astype(F32)
        for d in range(3):
            total = total + cy_recv[i, d].astype(F32)
        sum_rows[...] = total
        for zz in range(NZ):
            for k in range(3):
                z_rows[zz, 4 * k : 4 * k + 4] = sum_rows[k, 4 * zz : 4 * zz + 4]
        cz_send[i] = z_rows[...].astype(BF)
        return [
            send(CONV_Z + 7 * i + d - 1, cz_send.at[i, (z + d) % NZ], cz_recv.at[i, d - 1], zs[d - 1])
            for d in range(1, NZ)
        ]

    conv_z = {}
    conv_z[1] = conv_after_y(1)

    for copy in down_n:
        copy.wait_recv()
    total = dn_send[pl.ds(l, 1), pl.ds(c, 1)].reshape(32, 16, 128).astype(F32)
    for d in range(3):
        total = total + dn_recv[d].astype(F32)
    dy_send[...] = total.reshape(NY, NZ, 16, 128).astype(BF)
    down_y = [
        send(DOWN_Y + d - 1, dy_send.at[(y + d) % NY], dy_recv.at[d - 1], ys[d - 1]) for d in range(1, NY)
    ]

    conv_z[0] = conv_after_y(0)

    for copy in act_copies:
        copy.wait_recv()
    for m in range(4):
        act_out[256 * m : 256 * m + 128] = act_recv[m][:, :64]
        act_out[256 * m + 128 : 256 * m + 256] = act_recv[m][:, 64:]

    conv_z[2] = conv_after_y(2)

    for copy in down_y:
        copy.wait_recv()
    total = dy_send[pl.ds(y, 1)].reshape(NZ, 16, 128).astype(F32)
    for d in range(3):
        total = total + dy_recv[d].astype(F32)
    dz_send[...] = total.astype(BF)
    down_z = [
        send(DOWN_Z + d - 1, dz_send.at[(z + d) % NZ], dz_recv.at[d - 1], zs[d - 1]) for d in range(1, NZ)
    ]

    for i in (1, 0, 2):
        for copy in conv_z[i]:
            copy.wait_recv()
        total = cz_send[pl.ds(i, 1), pl.ds(z, 1)].reshape(16, 384).astype(F32)
        for d in range(7):
            total = total + cz_recv[i, d].astype(F32)
        last_send[:, 384 * i : 384 * i + 384] = total.astype(BF)
    for copy in down_z:
        copy.wait_recv()
    total = dz_send[pl.ds(z, 1)].reshape(16, 128).astype(F32)
    for d in range(7):
        total = total + dz_recv[d].astype(F32)
    last_send[:, 1152:1280] = total.astype(BF)
    last_copies = [send(LAST + s, last_send, last_recv.at[s], lasts[s]) for s in range(3)]
    for copy in last_copies:
        copy.wait_recv()

    same = last_send[...].astype(F32) + last_recv[0].astype(F32)
    crossed = last_recv[2].astype(F32) + last_recv[1].astype(F32)
    conv = jnp.where(c == xh, same, crossed) * factor
    for s in range(9):
        own = jnp.where(c == 0, conv[:, 128 * s : 128 * s + 64], conv[:, 128 * s + 64 : 128 * s + 128])
        for k in range(3):
            cg_out[3 * s + k] = own[4 * k : 4 * k + 4]
    same, crossed = same[:, 1152:], crossed[:, 1152:]
    both = jnp.concatenate(
        [jnp.where(c == 0, same, crossed), jnp.where(c == 0, crossed, same)], axis=1
    )
    mine = jnp.zeros((4, 256), F32)
    for s in range(4):
        mine = mine + jnp.where(2 * xh + c == s, both[4 * s : 4 * s + 4], 0.0)
    dg_out[...] = mine * factor

    for copy in started:
        copy.wait_send()


def on_device(volume, down_weight, conv_weight, cotangent):
    factor = 1.0 / (32 * math.sqrt(64))
    hbm = pl.BlockSpec(memory_space=pl.ANY)
    vmem = pl.BlockSpec(memory_space=pltpu.VMEM)
    scratch = [
        ((2, 8, 2, 64, 128), BF),
        ((1024, 256), BF),
        ((27, 256, 256), BF),
        ((4, 256, 64), BF),
        ((2, 8, 2, 64, 128), F32),
        ((256, 1024), BF),
        ((1024, 256), BF),
        ((2, 3, 10, 32, 128), BF),
        ((2, 3, 10, 32, 128), BF),
        ((3, 34, 32, 128), BF),
        ((2, 128, 256), BF),
        ((4, 128, 256), BF),
        ((384, 1024), BF),
        ((3, 256, 256), F32),
        ((4, 128, 128), BF),
        ((4, 128, 128), BF),
        ((4, 128, 128), BF),
        ((4, 128, 128), BF),
        ((3, 4, 3, 32, 384), BF),
        ((3, 3, 3, 32, 384), BF),
        ((3, 32, 384), F32),
        ((8, 16, 384), F32),
        ((3, 8, 16, 384), BF),
        ((3, 7, 16, 384), BF),
        ((2, 2, 32, 16, 128), F32),
        ((2, 2, 32, 16, 128), BF),
        ((3, 32, 16, 128), BF),
        ((4, 8, 16, 128), BF),
        ((3, 8, 16, 128), BF),
        ((8, 16, 128), BF),
        ((7, 16, 128), BF),
        ((16, 1280), BF),
        ((3, 16, 1280), BF),
    ]
    activated, volume_grad, down_grad, conv_grad = pl.pallas_call(
        functools.partial(kernel, factor),
        name="unet_level",
        out_shape=(
            jax.ShapeDtypeStruct((1024, 64), BF),
            jax.ShapeDtypeStruct((2, 8, 2, 64, 128), BF),
            jax.ShapeDtypeStruct((4, 256), F32),
            jax.ShapeDtypeStruct((27, 4, 64), F32),
        ),
        in_specs=[hbm] * 4,
        out_specs=(vmem,) * 4,
        scratch_shapes=[pltpu.VMEM(shape, dtype) for shape, dtype in scratch]
        + [
            pltpu.SemaphoreType.DMA((4,)),
            pltpu.SemaphoreType.DMA((MESSAGES,)),
            pltpu.SemaphoreType.DMA((MESSAGES,)),
        ],
        compiler_params=pltpu.CompilerParams(
            collective_id=0, has_side_effects=True, vmem_limit_bytes=48 * 1024 * 1024
        ),
        cost_estimate=pl.CostEstimate(flops=3200000000, bytes_accessed=8000000, transcendentals=65536),
    )(
        volume.reshape(2, 8, 2, 64, 128),
        down_weight,
        conv_weight,
        cotangent.reshape(4, 256, 64),
    )
    return (
        activated.reshape(1, 32, 32, 64),
        volume_grad.reshape(2, 16, 64, 128),
        down_grad,
        conv_grad.transpose(0, 2, 1),
    )


def solution(mesh):
    placed = (P("wide", "narrow", None, None), P(), P(), P("wide", None, None, "narrow"))
    return jax.shard_map(
        on_device,
        mesh=mesh,
        in_specs=placed,
        out_specs=(
            P("wide", None, None, "narrow"),
            P("wide", "narrow", None, None),
            P(("wide", "narrow"), None),
            P(None, "narrow", "wide"),
        ),
        check_vma=False,
    )
```

time: 931 us -> 69.7 us (0.07)
  the two profiles are of different devices: /device:TPU:2 before, /device:TPU:1 now
where the time goes in v1:
time: 69.7 us; the launch traced here: 69.4 us
  Pallas kernels  61 us (88%)
  local copies, waits for them, and re-layouts  7.74 us (11%)
    pallas_call x1, Pallas kernels, on_device(): pl.pallas_call(functools.partial(kernel, factor), name='unet_level', out_...  61 us
    unnamed x12, local copies, waits for them, and re-layouts  7.74 us

profile of v1, /device:TPU:1, one launch (start us, length us, event | category | flops | bytes accessed | tf_op | source)
XLA Modules:
  0.0 69.4 jit_solution(10718256241213543828)
XLA Ops:
  0.6 0.0 copy-start
  0.6 2.0 %copy-done = bf16[27,256,256]{2,1,0:T(8,128)(2,1)S(1)} copy-done((bf16[27,256,256]{2,1,0:T(8,128)(2,1)S(1)}, bf16[27,256,256]{2,1,0:T(8,128)(2,1)}, u32[]{:S(2)}) %copy-start) | copy-done | bytes 3538968
  2.6 0.0 copy-start.1
  2.6 1.0 %copy-done.1 = bf16[2,16,64,128]{3,2,1,0:T(8,128)(2,1)S(1)} copy-done((bf16[2,16,64,128]{3,2,1,0:T(8,128)(2,1)S(1)}, bf16[2,16,64,128]{3,2,1,0:T(8,128)(2,1)}, u32[]{:S(2)}) %copy-start.1) | copy-done | bytes 524312
  3.7 0.0 copy-start.2
  3.7 1.0 %copy-done.2 = bf16[1024,256]{1,0:T(8,128)(2,1)S(1)} copy-done((bf16[1024,256]{1,0:T(8,128)(2,1)S(1)}, bf16[1024,256]{1,0:T(8,128)(2,1)}, u32[]{:S(2)}) %copy-start.2) | copy-done | bytes 524312
  4.7 0.0 copy-start.3
  4.7 0.9 %copy-done.3 = bf16[1,32,32,64]{3,2,1,0:T(8,128)(2,1)S(1)} copy-done((bf16[1,32,32,64]{3,2,1,0:T(8,128)(2,1)S(1)}, bf16[1,32,32,64]{3,2,1,0:T(8,128)(2,1)}, u32[]{:S(2)}) %copy-start.3) | copy-done | bytes 131096
  5.7 61.0 %unet_level.1 = (bf16[1024,64]{1,0:T(8,128)(2,1)S(1)}, bf16[2,8,2,64,128]{4,3,2,1,0:T(8,128)(2,1)S(1)}, f32[4,256]{1,0:T(4,128)S(1)}, f32[27,4,64]{2,1,0:T(4,128)S(1)}) custom-call(bf16[2,8,2,64,128]{4,3,2,1,0:T(8,128)(2,1)S(1)} %bitcast.8, bf16[1024,256]{1,0:T(8,128)(2,1)S(1)} %copy-done.2, bf16[27,256,256]{2,1,0:T(8,128)(2,1)S(1)} %copy-done, ...), custom_call_target="tpu_custom_call" | custom-call | flops 3200000000 | bytes 8000000 | tf_op jit(solution)/shard_map/unet_level/pallas_call | solution.py:457
  66.7 0.7 %copy.12 = bf16[1,32,32,64]{3,2,1,0:T(8,128)(2,1)} copy(bf16[1,32,32,64]{3,2,1,0:T(8,128)(2,1)S(1)} %bitcast.6) | data formatting | bytes 262144
  67.4 0.8 %copy.13 = bf16[2,16,64,128]{3,2,1,0:T(8,128)(2,1)} copy(bf16[2,16,64,128]{3,2,1,0:T(8,128)(2,1)S(1)} %bitcast.5) | data formatting | bytes 1048576
  68.2 0.6 copy.14
  68.8 0.6 copy.15
Async XLA Ops:
  0.6 2.0 %copy-start = (bf16[27,256,256]{2,1,0:T(8,128)(2,1)S(1)}, bf16[27,256,256]{2,1,0:T(8,128)(2,1)}, u32[]{:S(2)}) copy-start(bf16[27,256,256]{2,1,0:T(8,128)(2,1)} %cw_ref.1) | copy-start | bytes 10616836
  2.6 1.0 %copy-start.1 = (bf16[2,16,64,128]{3,2,1,0:T(8,128)(2,1)S(1)}, bf16[2,16,64,128]{3,2,1,0:T(8,128)(2,1)}, u32[]{:S(2)}) copy-start(bf16[2,16,64,128]{3,2,1,0:T(8,128)(2,1)} %param.4) | copy-start | bytes 1572868
  3.7 1.0 %copy-start.2 = (bf16[1024,256]{1,0:T(8,128)(2,1)S(1)}, bf16[1024,256]{1,0:T(8,128)(2,1)}, u32[]{:S(2)}) copy-start(bf16[1024,256]{1,0:T(8,128)(2,1)} %dw_ref.1) | copy-start | bytes 1572868
  4.7 0.9 %copy-start.3 = (bf16[1,32,32,64]{3,2,1,0:T(8,128)(2,1)S(1)}, bf16[1,32,32,64]{3,2,1,0:T(8,128)(2,1)}, u32[]{:S(2)}) copy-start(bf16[1,32,32,64]{3,2,1,0:T(8,128)(2,1)} %param.7) | copy-start | bytes 393220

commit v2 on v1

--- a/solution.py
+++ b/solution.py
@@ -21,11 +21,13 @@
 GRAD_SHARE = 31
 CONV_Y = 34
 CONV_Z = 43
-DOWN_N = 64
-DOWN_Y = 67
-DOWN_Z = 70
-LAST = 77
-MESSAGES = 80
+DOWN_C = 64
+DOWN_X = 65
+DOWN_Y = 68
+DOWN_Z = 71
+DOWN_LAST = 78
+CONV_LAST = 79
+MESSAGES = 82
 
 
 def matmul(a, b):
@@ -70,13 +72,17 @@
     z_rows,
     cz_send,
     cz_recv,
-    dn_rows,
-    dn_send,
-    dn_recv,
+    dc_send,
+    dc_recv,
+    dx_rows,
+    dx_send,
+    dx_recv,
     dy_send,
     dy_recv,
     dz_send,
     dz_recv,
+    dl_send,
+    dl_recv,
     last_send,
     last_recv,
     local_sem,
@@ -98,17 +104,20 @@
     ys = [(wide_of(y + d, z, xh), n) for d in range(1, NY)]
     zs = [(wide_of(y, z + d, xh), n) for d in range(1, NZ)]
     other_c = n + 1 - 2 * c
-    lasts = [(wide_of(y, z, 1 - xh), n), (wide_of(y, z, 1 - xh), other_c), (w, other_c)]
+    across = wide_of(y, z, 1 - xh)
+    other_l = (n + 2) % 4
+    xs = [(across, n), (w, other_l), (across, other_l)]
+    lasts = [(across, n), (across, other_c), (w, other_c)]
 
     barrier = pltpu.get_barrier_semaphore()
-    partners = near + depth + ys + zs + lasts[:2]
+    partners = near + depth + ys + zs + [(across, n), (across, other_c), (across, other_l)]
     for who in partners:
         pl.semaphore_signal(barrier, inc=1, device_id=who, device_id_type=MESH)
 
     started = []
 
-    def send(number, src, dst, who):
-        copy = pltpu.make_async_remote_copy(
+    def remote(number, src, dst, who):
+        return pltpu.make_async_remote_copy(
             src_ref=src,
             dst_ref=dst,
             send_sem=send_sem.at[number],
@@ -116,6 +125,9 @@
             device_id=who,
             device_id_type=MESH,
         )
+
+    def send(number, src, dst, who):
+        copy = remote(number, src, dst, who)
         copy.start()
         started.append(copy)
         return copy
@@ -130,28 +142,6 @@
     deep_all[:, 0:1] = jnp.zeros((3, 1, 32, 128), BF)
     deep_all[:, 33:34] = jnp.zeros((3, 1, 32, 128), BF)
     z_rows[...] = jnp.zeros_like(z_rows)
-
-    loads[0].wait()
-    for m in range(4):
-        cot_send[m] = jnp.concatenate([cot[m, :128], cot[m, 128:]], axis=1)
-    cot_recv[pl.ds(n, 1)] = cot_send[pl.ds(n, 1)]
-    pl.semaphore_wait(barrier, len(partners))
-    cot_copies = [
-        send(COT + d - 1, cot_send.at[(n + d) % 4], cot_recv.at[n], near[d - 1]) for d in range(1, 4)
-    ]
-
-    loads[1].wait()
-    wide_f32[...] = vol[...].astype(F32)
-    for a in range(2):
-        for b in range(2):
-            for e in range(2):
-                part = wide_f32[a, :, b, pl.ds(e, 32, stride=2), :].reshape(256, 128).astype(BF)
-                at = (4 * a + 2 * b + e) * 128
-                patches[:, at : at + 128] = part
-    loads[2].wait()
-    cells = matmul(patches[...], dw[...]).astype(BF)
-    for half in range(2):
-        deep[half, 1, 1:9] = cells[:, 128 * half : 128 * half + 128].reshape(8, 32, 128)
 
     def send_halos(buf, base):
         copies = []
@@ -189,20 +179,49 @@
         def _():
             buf[:, plane] = jnp.zeros((2, 10, 32, 128), BF)
 
+    loads[0].wait()
+    for m in range(4):
+        cot_send[m] = jnp.concatenate([cot[m, :128], cot[m, 128:]], axis=1)
+    cot_recv[pl.ds(n, 1)] = cot_send[pl.ds(n, 1)]
+    loads[1].wait()
+    wide_f32[...] = vol[...].astype(F32)
+    for a in range(2):
+        for b in range(2):
+            for e in range(2):
+                part = wide_f32[a, :, b, pl.ds(e, 32, stride=2), :].reshape(256, 128).astype(BF)
+                at = (4 * a + 2 * b + e) * 128
+                patches[:, at : at + 128] = part
+    loads[2].wait()
+    cells = matmul(patches[...], dw[...]).astype(BF)
+    for half in range(2):
+        deep[half, 1, 1:9] = cells[:, 128 * half : 128 * half + 128].reshape(8, 32, 128)
+
     def share_deep(plane):
-        deep_all[plane, pl.ds(1 + 8 * n, 8)] = deep[pl.ds(l, 1), plane, 1:9].reshape(8, 32, 128)
+        mine = pl.ds(1 + 8 * n, 8)
+        deep_all[plane, mine] = deep[pl.ds(l, 1), plane, 1:9].reshape(8, 32, 128)
         return [
+            send(DEEP_SHARE + 3 * plane, deep.at[1 - l, plane, pl.ds(1, 8)], deep_all.at[plane, mine], (w, other_l)),
+            send(DEEP_SHARE + 3 * plane + 1, deep.at[l, plane, pl.ds(1, 8)], deep_all.at[plane, mine], (w, other_c)),
+        ]
+
+    def pass_on(plane):
+        shared[plane][0].wait_recv()
+        theirs = pl.ds(1 + 8 * other_l, 8)
+        shared[plane].append(
             send(
-                DEEP_SHARE + 3 * plane + d - 1,
-                deep.at[((n + d) % 4) // 2, plane, pl.ds(1, 8)],
-                deep_all.at[plane, pl.ds(1 + 8 * n, 8)],
-                near[d - 1],
+                DEEP_SHARE + 3 * plane + 2,
+                deep_all.at[plane, theirs],
+                deep_all.at[plane, theirs],
+                (w, other_c),
             )
-            for d in range(1, 4)
-        ]
-
+        )
+
+    pl.semaphore_wait(barrier, len(partners))
     deep_halos = send_halos(deep, DEEP_HALO)
-    shared = {1: share_deep(1)}
+    cot_copies = [
+        send(COT + d - 1, cot_send.at[(n + d) % 4], cot_recv.at[n], near[d - 1]) for d in range(1, 4)
+    ]
+    shared = {}
     for s in range(4):
         block = patches[:, 256 * s : 256 * s + 256].astype(F32)
         patches_t[256 * s : 256 * s + 256, :] = block.T.astype(BF)
@@ -226,6 +245,8 @@
             weights = jnp.concatenate([cw[9 * i + 3 * j + k] for j in range(3)], axis=0)
             term = matmul(slab, weights)
             acc[k] = term if i == 1 else acc[k] + term
+        if i == 1:
+            shared[1] = share_deep(1)
     preact = shifted(acc[0], 1, 0) + acc[1] + shifted(acc[2], 255, 31)
 
     for copy in cot_copies:
@@ -258,13 +279,8 @@
     ]
     grad_halos = send_halos(grad, GRAD_HALO)
 
-    for m in range(4):
-        part = activated[:, 64 * m : 64 * m + 64]
-        act_send[m] = jnp.concatenate([part[:128], part[128:]], axis=1)
-    act_recv[pl.ds(n, 1)] = act_send[pl.ds(n, 1)]
-    act_copies = [
-        send(ACT + d - 1, act_send.at[(n + d) % 4], act_recv.at[n], near[d - 1]) for d in range(1, 4)
-    ]
+    for i in (1, 0, 2):
+        pass_on(i)
 
     for copy in grad_shared:
         copy.wait_recv()
@@ -277,7 +293,7 @@
         grad_rows[256:384, at : at + 256] = jnp.where(lane == 0, 0.0, pltpu.roll(block, 1, 1)).astype(BF)
     conv_y = {}
     for i in (1, 0, 2):
-        for copy in shared[i]:
+        for copy in shared[i][1:]:
             copy.wait_recv()
         slab = jnp.concatenate([deep_all[i, j : j + 32].reshape(1024, 128) for j in range(3)], axis=1)
         term = matmul(grad_rows[...], slab).astype(BF)
@@ -305,20 +321,18 @@
             acc[k] = term if i == 1 else acc[k] + term
     grad_deep = (shifted(acc[0], 255, 31) + acc[1] + shifted(acc[2], 1, 0)).astype(BF)
 
-    partial = matmul(patches_t[...], grad_deep).reshape(32, 2, 2, 8, 256)
-    for ll in range(2):
-        for cc in range(2):
-            for xx in range(2):
-                dn_rows[ll, cc, :, 8 * xx : 8 * xx + 8] = partial[:, xx, ll, :, 128 * cc : 128 * cc + 128]
-    dn_send[...] = dn_rows[...].astype(BF)
-    down_n = [
-        send(
-            DOWN_N + d - 1,
-            dn_send.at[((n + d) % 4) // 2, (n + d) % 2],
-            dn_recv.at[d - 1],
-            near[d - 1],
-        )
-        for d in range(1, 4)
+    partial = matmul(patches_t[...], grad_deep)
+    low, high = partial[:, :128], partial[:, 128:]
+    dc_send[...] = jnp.where(c == 0, high, low).astype(BF)
+    down_c = send(DOWN_C, dc_send, dc_recv, (w, other_c))
+    kept = jnp.where(c == 0, low, high)
+
+    for m in range(4):
+        part = activated[:, 64 * m : 64 * m + 64]
+        act_send[m] = jnp.concatenate([part[:128], part[128:]], axis=1)
+    act_recv[pl.ds(n, 1)] = act_send[pl.ds(n, 1)]
+    act_copies = [
+        send(ACT + d - 1, act_send.at[(n + d) % 4], act_recv.at[n], near[d - 1]) for d in range(1, 4)
     ]
 
     spread = matmul_nt(grad_deep, dw[...])
@@ -345,20 +359,34 @@
             for d in range(1, NZ)
         ]
 
+    down_c.wait_recv()
+    total = (kept + dc_recv[...].astype(F32)).reshape(16, 2, 2, 2, 8, 128)
+    for xx in range(2):
+        for ll in range(2):
+            for zz in range(2):
+                dx_rows[xx, ll, :, 8 * zz : 8 * zz + 8] = total[:, zz, xx, ll]
+    dx_send[...] = dx_rows[...].astype(BF)
+    down_x = [
+        send(DOWN_X + s, dx_send.at[xx, ll], dx_recv.at[s], xs[s])
+        for s, (xx, ll) in enumerate(((1 - xh, l), (xh, 1 - l), (1 - xh, 1 - l)))
+    ]
+
     conv_z = {}
     conv_z[1] = conv_after_y(1)
 
-    for copy in down_n:
+    conv_z[0] = conv_after_y(0)
+
+    conv_z[2] = conv_after_y(2)
+
+    for copy in down_x:
         copy.wait_recv()
-    total = dn_send[pl.ds(l, 1), pl.ds(c, 1)].reshape(32, 16, 128).astype(F32)
+    total = dx_rows[pl.ds(xh, 1), pl.ds(l, 1)].reshape(16, 16, 128)
     for d in range(3):
-        total = total + dn_recv[d].astype(F32)
-    dy_send[...] = total.reshape(NY, NZ, 16, 128).astype(BF)
+        total = total + dx_recv[d].astype(F32)
+    dy_send[...] = total.reshape(NY, 4, 16, 128).astype(BF)
     down_y = [
         send(DOWN_Y + d - 1, dy_send.at[(y + d) % NY], dy_recv.at[d - 1], ys[d - 1]) for d in range(1, NY)
     ]
-
-    conv_z[0] = conv_after_y(0)
 
     for copy in act_copies:
         copy.wait_recv()
@@ -366,14 +394,12 @@
         act_out[256 * m : 256 * m + 128] = act_recv[m][:, :64]
         act_out[256 * m + 128 : 256 * m + 256] = act_recv[m][:, 64:]
 
-    conv_z[2] = conv_after_y(2)
-
     for copy in down_y:
         copy.wait_recv()
-    total = dy_send[pl.ds(y, 1)].reshape(NZ, 16, 128).astype(F32)
+    total = dy_send[pl.ds(y, 1)].reshape(4, 16, 128).astype(F32)
     for d in range(3):
         total = total + dy_recv[d].astype(F32)
-    dz_send[...] = total.astype(BF)
+    dz_send[...] = total.reshape(NZ, 8, 128)
     down_z = [
         send(DOWN_Z + d - 1, dz_send.at[(z + d) % NZ], dz_recv.at[d - 1], zs[d - 1]) for d in range(1, NZ)
     ]
@@ -385,39 +411,64 @@
         for d in range(7):
             total = total + cz_recv[i, d].astype(F32)
         last_send[:, 384 * i : 384 * i + 384] = total.astype(BF)
+    @pl.when(xh == c)
+    def _():
+        copy = remote(CONV_LAST + 2, last_send, last_recv.at[2], (w, other_c))
+        copy.start()
+        remote(CONV_LAST, last_send, last_recv.at[0], (across, n)).wait_recv()
+        copy.wait_send()
+
+    @pl.when(xh != c)
+    def _():
+        one = remote(CONV_LAST, last_send, last_recv.at[0], (across, n))
+        two = remote(CONV_LAST + 1, last_send, last_recv.at[1], (across, other_c))
+        one.start()
+        two.start()
+        two.wait_recv()
+        remote(CONV_LAST + 2, last_send, last_recv.at[2], (w, other_c)).wait_recv()
+        one.wait_send()
+        two.wait_send()
+
     for copy in down_z:
         copy.wait_recv()
-    total = dz_send[pl.ds(z, 1)].reshape(16, 128).astype(F32)
+    total = dz_send[pl.ds(z, 1)].reshape(8, 128)
     for d in range(7):
-        total = total + dz_recv[d].astype(F32)
-    last_send[:, 1152:1280] = total.astype(BF)
-    last_copies = [send(LAST + s, last_send, last_recv.at[s], lasts[s]) for s in range(3)]
-    for copy in last_copies:
-        copy.wait_recv()
-
-    same = last_send[...].astype(F32) + last_recv[0].astype(F32)
-    crossed = last_recv[2].astype(F32) + last_recv[1].astype(F32)
-    conv = jnp.where(c == xh, same, crossed) * factor
+        total = total + dz_recv[d]
+    dl_send[...] = total
+    down_last = send(DOWN_LAST, dl_send, dl_recv, (w, other_c))
+
+    one = jnp.where(c == xh, last_send[...], last_recv[2])
+    two = jnp.where(c == xh, last_recv[0], last_recv[1])
+    conv = (one.astype(F32) + two.astype(F32)) * factor
     for s in range(9):
         own = jnp.where(c == 0, conv[:, 128 * s : 128 * s + 64], conv[:, 128 * s + 64 : 128 * s + 128])
         for k in range(3):
             cg_out[3 * s + k] = own[4 * k : 4 * k + 4]
-    same, crossed = same[:, 1152:], crossed[:, 1152:]
-    both = jnp.concatenate(
-        [jnp.where(c == 0, same, crossed), jnp.where(c == 0, crossed, same)], axis=1
-    )
-    mine = jnp.zeros((4, 256), F32)
-    for s in range(4):
-        mine = mine + jnp.where(2 * xh + c == s, both[4 * s : 4 * s + 4], 0.0)
-    dg_out[...] = mine * factor
+    down_last.wait_recv()
+    theirs = dl_recv[...]
+    both = jnp.concatenate([jnp.where(c == 0, total, theirs), jnp.where(c == 0, theirs, total)], axis=1)
+    dg_out[...] = jnp.where(c == 0, both[:4], both[4:]) * factor
 
     for copy in started:
         copy.wait_send()
 
 
+def write_out(*refs):
+    arrays = (len(refs) - 1) // 2
+    sems = refs[-1]
+    copies = [
+        pltpu.make_async_copy(src, dst, sems.at[s])
+        for s, (src, dst) in enumerate(zip(refs[:arrays], refs[arrays:-1]))
+    ]
+    for copy in copies:
+        copy.start()
+    for copy in copies:
+        copy.wait()
+
+
 def on_device(volume, down_weight, conv_weight, cotangent):
     factor = 1.0 / (32 * math.sqrt(64))
-    hbm = pl.BlockSpec(memory_space=pl.ANY)
+    hbm = pl.BlockSpec(memory_space=pltpu.HBM)
     vmem = pl.BlockSpec(memory_space=pltpu.VMEM)
     scratch = [
         ((2, 8, 2, 64, 128), BF),
@@ -444,17 +495,21 @@
         ((8, 16, 384), F32),
         ((3, 8, 16, 384), BF),
         ((3, 7, 16, 384), BF),
-        ((2, 2, 32, 16, 128), F32),
-        ((2, 2, 32, 16, 128), BF),
-        ((3, 32, 16, 128), BF),
-        ((4, 8, 16, 128), BF),
-        ((3, 8, 16, 128), BF),
-        ((8, 16, 128), BF),
-        ((7, 16, 128), BF),
-        ((16, 1280), BF),
-        ((3, 16, 1280), BF),
-    ]
-    activated, volume_grad, down_grad, conv_grad = pl.pallas_call(
+        ((1024, 128), BF),
+        ((1024, 128), BF),
+        ((2, 2, 16, 16, 128), F32),
+        ((2, 2, 16, 16, 128), BF),
+        ((3, 16, 16, 128), BF),
+        ((4, 4, 16, 128), BF),
+        ((3, 4, 16, 128), BF),
+        ((8, 8, 128), F32),
+        ((7, 8, 128), F32),
+        ((8, 128), F32),
+        ((8, 128), F32),
+        ((16, 1152), BF),
+        ((3, 16, 1152), BF),
+    ]
+    results = pl.pallas_call(
         functools.partial(kernel, factor),
         name="unet_level",
         out_shape=(
@@ -472,7 +527,7 @@
             pltpu.SemaphoreType.DMA((MESSAGES,)),
         ],
         compiler_params=pltpu.CompilerParams(
-            collective_id=0, has_side_effects=True, vmem_limit_bytes=48 * 1024 * 1024
+            collective_id=0, has_side_effects=True, vmem_limit_bytes=56 * 1024 * 1024
         ),
         cost_estimate=pl.CostEstimate(flops=3200000000, bytes_accessed=8000000, transcendentals=65536),
     )(
@@ -481,6 +536,14 @@
         conv_weight,
         cotangent.reshape(4, 256, 64),
     )
+    activated, volume_grad, down_grad, conv_grad = pl.pallas_call(
+        write_out,
+        name="write_out",
+        out_shape=tuple(jax.ShapeDtypeStruct(r.shape, r.dtype) for r in results),
+        in_specs=[vmem] * 4,
+        out_specs=(hbm,) * 4,
+        scratch_shapes=[pltpu.SemaphoreType.DMA((4,))],
+    )(*results)
     return (
         activated.reshape(1, 32, 32, 64),
         volume_grad.reshape(2, 16, 64, 128),

time: 69.7 us -> 59.1 us (0.85)
  local copies, waits for them, and re-layouts: 7.74 us -> 0 us
  Pallas kernels: 61 us -> 58.4 us
    unnamed x12 -> x0, local copies, waits for them, and re-layouts: 7.74 us -> none
    pallas_call x1, Pallas kernels: 61 us -> 56.3 us  [on_device(): pl.pallas_call(functools.partial(kernel, factor), name='unet_level', out_...]
    pallas_call x0 -> x1, Pallas kernels: none -> 2.03 us  [on_device(): pl.pallas_call(write_out, name='write_out', out_shape=tuple((jax.ShapeDty...]
where the time goes in v2:
time: 59.1 us; the launch traced here: 59 us
  Pallas kernels  58.4 us (99%)
  between operations  0.64 us (1%)
    pallas_call x1, Pallas kernels, on_device(): pl.pallas_call(functools.partial(kernel, factor), name='unet_level', out_...  56.3 us
    pallas_call x1, Pallas kernels, on_device(): pl.pallas_call(write_out, name='write_out', out_shape=tuple((jax.ShapeDty...  2.03 us

profile of v2, /device:TPU:1, one launch (start us, length us, event | category | flops | bytes accessed | tf_op | source)
XLA Modules:
  0.0 59.0 jit_solution(15276271986222428489)
XLA Ops:
  0.6 56.3 %unet_level.1 = (bf16[1024,64]{1,0:T(8,128)(2,1)}, bf16[2,8,2,64,128]{4,3,2,1,0:T(8,128)(2,1)}, f32[4,256]{1,0:T(4,128)}, f32[27,4,64]{2,1,0:T(4,128)}) custom-call(bf16[2,8,2,64,128]{4,3,2,1,0:T(8,128)(2,1)} %bitcast.5, bf16[1024,256]{1,0:T(8,128)(2,1)} %dw_ref.1, bf16[27,256,256]{2,1,0:T(8,128)(2,1)} %cw_ref.1, bf16[4,256,64]{2,1,0:T(8,128)(2,1)} %bitcast.7), custom_call_target="tpu_custom_call" | custom-call | flops 3200000000 | bytes 8000000 | tf_op jit(solution)/shard_map/unet_level/pallas_call | solution.py:512
  57.0 2.0 %write_out.1 = (bf16[1024,64]{1,0:T(8,128)(2,1)}, bf16[2,8,2,64,128]{4,3,2,1,0:T(8,128)(2,1)}, f32[4,256]{1,0:T(4,128)}, f32[27,4,64]{2,1,0:T(4,128)}) custom-call(bf16[1024,64]{1,0:T(8,128)(2,1)} %get-tuple-element.12.refs_0_, bf16[2,8,2,64,128]{4,3,2,1,0:T(8,128)(2,1)} %get-tuple-element.13.refs_1_, f32[4,256]{1,0:T(4,128)} %get-tuple-element.14.refs_2_, ...), custom_call_target="tpu_custom_call" | custom-call | tf_op jit(solution)/shard_map/write_out/pallas_call | solution.py:539

commit v3 on v2

--- a/solution.py
+++ b/solution.py
@@ -15,19 +15,22 @@
 
 COT = 0
 DEEP_HALO = 3
-DEEP_SHARE = 11
+DEEP_ACROSS = 11
+DEEP_CORE = 13
 ACT = 20
 GRAD_HALO = 23
 GRAD_SHARE = 31
-CONV_Y = 34
-CONV_Z = 43
-DOWN_C = 64
-DOWN_X = 65
-DOWN_Y = 68
-DOWN_Z = 71
-DOWN_LAST = 78
-CONV_LAST = 79
-MESSAGES = 82
+CONV_Y = 35
+CONV_YZ = 38
+CONV_Z = 45
+CONV_ZY = 52
+DOWN_C = 55
+DOWN_X = 56
+DOWN_Y = 59
+DOWN_Z = 62
+DOWN_LAST = 69
+CONV_LAST = 70
+MESSAGES = 76
 
 
 def matmul(a, b):
@@ -61,6 +64,7 @@
     grad_t_send,
     grad_t,
     grad_rows,
+    grad_rows_z,
     acc,
     cot_send,
     cot_recv,
@@ -69,9 +73,14 @@
     cy_send,
     cy_recv,
     sum_rows,
-    z_rows,
+    cyz_rows,
+    cyz_send,
+    cyz_recv,
     cz_send,
     cz_recv,
+    czy_rows,
+    czy_send,
+    czy_recv,
     dc_send,
     dc_recv,
     dx_rows,
@@ -83,6 +92,7 @@
     dz_recv,
     dl_send,
     dl_recv,
+    last_sum,
     last_send,
     last_recv,
     local_sem,
@@ -93,6 +103,7 @@
     n = lax.axis_index("narrow")
     y, z, xh = w // 16, (w // 2) % NZ, w % 2
     l, c = n // 2, n % 2
+    pair = z % 2
 
     def wide_of(yy, zz, xx):
         return ((yy % NY) * NZ + zz % NZ) * 2 + xx
@@ -100,17 +111,17 @@
     near = [(w, (n + d) % 4) for d in range(1, 4)]
     up, down = (w + 1) % 64, (w + 63) % 64
     right, left = (n + 1) % 4, (n + 3) % 4
-    depth = [(s, m) for s in (up, down) for m in (n, right, left)]
+    depth = [(s, (n + d) % 4) for s in (up, down) for d in range(4)]
     ys = [(wide_of(y + d, z, xh), n) for d in range(1, NY)]
     zs = [(wide_of(y, z + d, xh), n) for d in range(1, NZ)]
     other_c = n + 1 - 2 * c
     across = wide_of(y, z, 1 - xh)
     other_l = (n + 2) % 4
+    beside = wide_of(y, z + 1 - 2 * pair, xh)
     xs = [(across, n), (w, other_l), (across, other_l)]
-    lasts = [(across, n), (across, other_c), (w, other_c)]
 
     barrier = pltpu.get_barrier_semaphore()
-    partners = near + depth + ys + zs + [(across, n), (across, other_c), (across, other_l)]
+    partners = near + depth + ys + zs
     for who in partners:
         pl.semaphore_signal(barrier, inc=1, device_id=who, device_id_type=MESH)
 
@@ -139,9 +150,8 @@
     for copy in loads:
         copy.start()
 
-    deep_all[:, 0:1] = jnp.zeros((3, 1, 32, 128), BF)
-    deep_all[:, 33:34] = jnp.zeros((3, 1, 32, 128), BF)
-    z_rows[...] = jnp.zeros_like(z_rows)
+    cyz_rows[...] = jnp.zeros_like(cyz_rows)
+    czy_rows[...] = jnp.zeros_like(czy_rows)
 
     def send_halos(buf, base):
         copies = []
@@ -196,32 +206,37 @@
     for half in range(2):
         deep[half, 1, 1:9] = cells[:, 128 * half : 128 * half + 128].reshape(8, 32, 128)
 
-    def share_deep(plane):
-        mine = pl.ds(1 + 8 * n, 8)
-        deep_all[plane, mine] = deep[pl.ds(l, 1), plane, 1:9].reshape(8, 32, 128)
-        return [
-            send(DEEP_SHARE + 3 * plane, deep.at[1 - l, plane, pl.ds(1, 8)], deep_all.at[plane, mine], (w, other_l)),
-            send(DEEP_SHARE + 3 * plane + 1, deep.at[l, plane, pl.ds(1, 8)], deep_all.at[plane, mine], (w, other_c)),
-        ]
-
-    def pass_on(plane):
-        shared[plane][0].wait_recv()
-        theirs = pl.ds(1 + 8 * other_l, 8)
-        shared[plane].append(
-            send(
-                DEEP_SHARE + 3 * plane + 2,
-                deep_all.at[plane, theirs],
-                deep_all.at[plane, theirs],
-                (w, other_c),
-            )
-        )
+    from_rows, to_rows = pl.ds(c, 9), pl.ds(9 * c, 9)
+    outer, inner = 2 * pair, 2 - 2 * pair
+
+    def to_core(number, src, plane, chip):
+        return remote(DEEP_CORE + number, src, deep_all.at[plane, chip, to_rows], (w, other_c))
+
+    def share_core(plane):
+        deep_all[plane, pl.ds(pair, 1), to_rows] = deep[pl.ds(pair, 1), plane, from_rows]
+        copy = to_core(plane, deep.at[pair, plane, from_rows], plane, pair)
+        copy.start()
+        started.append(copy)
+        return copy
+
+    across_own = remote(
+        DEEP_ACROSS, deep.at[1 - pair, 1, from_rows], deep_all.at[1, pair, to_rows], (beside, n)
+    )
+    across_outer = remote(
+        DEEP_ACROSS + 1, deep.at[1 - pair, outer, from_rows], deep_all.at[outer, pair, to_rows], (beside, n)
+    )
+    theirs_own = deep_all.at[1, 1 - pair, to_rows]
+    theirs_outer = deep_all.at[inner, 1 - pair, to_rows]
+    pass_own = to_core(3, theirs_own, 1, 1 - pair)
+    pass_outer = to_core(4, theirs_outer, inner, 1 - pair)
+    inner_core = to_core(5, deep.at[pair, inner, from_rows], outer, 1 - pair)
 
     pl.semaphore_wait(barrier, len(partners))
     deep_halos = send_halos(deep, DEEP_HALO)
     cot_copies = [
         send(COT + d - 1, cot_send.at[(n + d) % 4], cot_recv.at[n], near[d - 1]) for d in range(1, 4)
     ]
-    shared = {}
+    shared = []
     for s in range(4):
         block = patches[:, 256 * s : 256 * s + 256].astype(F32)
         patches_t[256 * s : 256 * s + 256, :] = block.T.astype(BF)
@@ -239,14 +254,21 @@
             rows_arrive(deep, deep_halos, 1)
         else:
             plane_arrives(deep, deep_halos, i)
-            shared[i] = share_deep(i)
+        shared.append(share_core(i))
+        if i == 1:
+            across_own.start()
+        else:
+            @pl.when(outer == i)
+            def _():
+                across_outer.start()
+
         slab = jnp.concatenate(window(deep, i, 0) + window(deep, i, 1) + window(deep, i, 2), axis=1)
         for k in range(3):
             weights = jnp.concatenate([cw[9 * i + 3 * j + k] for j in range(3)], axis=0)
             term = matmul(slab, weights)
             acc[k] = term if i == 1 else acc[k] + term
-        if i == 1:
-            shared[1] = share_deep(1)
+    deep_all[pl.ds(outer, 1), pl.ds(1 - pair, 1), to_rows] = deep[pl.ds(pair, 1), pl.ds(inner, 1), from_rows]
+    inner_core.start()
     preact = shifted(acc[0], 1, 0) + acc[1] + shifted(acc[2], 255, 31)
 
     for copy in cot_copies:
@@ -272,15 +294,22 @@
     turned = matmul_nt(order, grad_pre).astype(BF)
     grad_t_send[0] = turned[:128]
     grad_t_send[1] = turned[128:]
-    grad_t[pl.ds(n, 1)] = grad_t_send[pl.ds(c, 1)]
+    slot = 2 * pair + c
+    grad_t[pl.ds(slot, 1)] = grad_t_send[pl.ds(c, 1)]
+    mine = grad_t.at[slot]
     grad_shared = [
-        send(GRAD_SHARE + d - 1, grad_t_send.at[(n + d) % 2], grad_t.at[n], near[d - 1])
-        for d in range(1, 4)
+        send(GRAD_SHARE, grad_t_send.at[1 - c], mine, (beside, other_c)),
+        send(GRAD_SHARE + 1, grad_t_send.at[c], mine, (beside, n)),
+        send(GRAD_SHARE + 2, grad_t_send.at[1 - c], mine, (w, other_c)),
     ]
     grad_halos = send_halos(grad, GRAD_HALO)
 
-    for i in (1, 0, 2):
-        pass_on(i)
+    across_own.wait_recv()
+    pass_own.start()
+    across_outer.wait_recv()
+    pass_outer.start()
+    started.extend([across_own, across_outer, pass_own, pass_outer, inner_core])
+    shared.extend([pass_own, pass_outer, inner_core])
 
     for copy in grad_shared:
         copy.wait_recv()
@@ -291,20 +320,35 @@
         grad_rows[0:128, at : at + 256] = jnp.where(lane == 31, 0.0, pltpu.roll(block, 255, 1)).astype(BF)
         grad_rows[128:256, at : at + 256] = grad_t[m]
         grad_rows[256:384, at : at + 256] = jnp.where(lane == 0, 0.0, pltpu.roll(block, 1, 1)).astype(BF)
-    conv_y = {}
-    for i in (1, 0, 2):
-        for copy in shared[i][1:]:
-            copy.wait_recv()
-        slab = jnp.concatenate([deep_all[i, j : j + 32].reshape(1024, 128) for j in range(3)], axis=1)
-        term = matmul(grad_rows[...], slab).astype(BF)
-        for yy in range(NY):
-            for k in range(3):
-                at = 128 * k + 32 * yy
-                cy_send[i, yy, k] = term[at : at + 32]
-        conv_y[i] = [
-            send(CONV_Y + 3 * i + d - 1, cy_send.at[i, (y + d) % NY], cy_recv.at[i, d - 1], ys[d - 1])
-            for d in range(1, NY)
-        ]
+    def cells_at(i, j):
+        return jnp.concatenate([deep_all[i, s, j : j + 16].reshape(512, 128) for s in range(2)], axis=0)
+
+    for copy in shared:
+        copy.wait_recv()
+    slab = jnp.concatenate([cells_at(i, j) for i in range(2) for j in range(3)], axis=1)
+    term = matmul(grad_rows[...], slab).astype(BF)
+    for yy in range(NY):
+        for k in range(3):
+            at = 128 * k + 32 * yy
+            cy_send[yy, k] = term[at : at + 32]
+    conv_y = [
+        send(CONV_Y + d - 1, cy_send.at[(y + d) % NY], cy_recv.at[d - 1], ys[d - 1]) for d in range(1, NY)
+    ]
+    row = lax.broadcasted_iota(jnp.int32, (128, 128), 0)
+    column = lax.broadcasted_iota(jnp.int32, (128, 128), 1)
+    source = ((row // 4) % 4) * 32 + (row // 16) * 4 + row % 4
+    order = jnp.where(column == source, 1.0, 0.0).astype(BF)
+    for k in range(3):
+        grad_rows_z[128 * k : 128 * k + 128, :] = matmul(order, grad_rows[128 * k : 128 * k + 128, :]).astype(BF)
+    slab = jnp.concatenate([cells_at(2, j) for j in range(3)], axis=1)
+    term = matmul(grad_rows_z[...], slab).astype(BF)
+    for zz in range(NZ):
+        for k in range(3):
+            at = 128 * k + 16 * zz
+            cz_send[zz, k] = term[at : at + 16]
+    conv_z = [
+        send(CONV_Z + d - 1, cz_send.at[(z + d) % NZ], cz_recv.at[d - 1], zs[d - 1]) for d in range(1, NZ)
+    ]
 
     for i in (1, 2, 0):
         plane = 2 - i
@@ -343,22 +387,6 @@
                 wide_f32[a, :, b, pl.ds(e, 32, stride=2), :] = spread[:, at : at + 128].reshape(8, 32, 128)
     vg_out[...] = wide_f32[...].astype(BF)
 
-    def conv_after_y(i):
-        for copy in conv_y[i]:
-            copy.wait_recv()
-        total = cy_send[pl.ds(i, 1), pl.ds(y, 1)].reshape(3, 32, 384).astype(F32)
-        for d in range(3):
-            total = total + cy_recv[i, d].astype(F32)
-        sum_rows[...] = total
-        for zz in range(NZ):
-            for k in range(3):
-                z_rows[zz, 4 * k : 4 * k + 4] = sum_rows[k, 4 * zz : 4 * zz + 4]
-        cz_send[i] = z_rows[...].astype(BF)
-        return [
-            send(CONV_Z + 7 * i + d - 1, cz_send.at[i, (z + d) % NZ], cz_recv.at[i, d - 1], zs[d - 1])
-            for d in range(1, NZ)
-        ]
-
     down_c.wait_recv()
     total = (kept + dc_recv[...].astype(F32)).reshape(16, 2, 2, 2, 8, 128)
     for xx in range(2):
@@ -371,12 +399,34 @@
         for s, (xx, ll) in enumerate(((1 - xh, l), (xh, 1 - l), (1 - xh, 1 - l)))
     ]
 
-    conv_z = {}
-    conv_z[1] = conv_after_y(1)
-
-    conv_z[0] = conv_after_y(0)
-
-    conv_z[2] = conv_after_y(2)
+    for copy in conv_y:
+        copy.wait_recv()
+    total = cy_send[pl.ds(y, 1)].reshape(3, 32, 768).astype(F32)
+    for d in range(3):
+        total = total + cy_recv[d].astype(F32)
+    sum_rows[...] = total
+    for zz in range(NZ):
+        for k in range(3):
+            cyz_rows[zz, 4 * k : 4 * k + 4] = sum_rows[k, 4 * zz : 4 * zz + 4]
+    cyz_send[...] = cyz_rows[...].astype(BF)
+    conv_yz = [
+        send(CONV_YZ + d - 1, cyz_send.at[(z + d) % NZ], cyz_recv.at[d - 1], zs[d - 1]) for d in range(1, NZ)
+    ]
+
+    for copy in conv_z:
+        copy.wait_recv()
+    halves = [cz_send[pl.ds(z, 1)].reshape(3, 16, 384).astype(F32), 0.0]
+    for d in range(1, NZ):
+        halves[d % 2] = halves[d % 2] + cz_recv[d - 1].astype(F32)
+    for h in range(2):
+        sum_rows[:, :16, :384] = halves[h]
+        for yy in range(NY):
+            for k in range(3):
+                czy_rows[yy, h, 4 * k : 4 * k + 4] = sum_rows[k, 4 * yy : 4 * yy + 4, :384]
+    czy_send[...] = czy_rows[...].astype(BF)
+    conv_zy = [
+        send(CONV_ZY + d - 1, czy_send.at[(y + d) % NY], czy_recv.at[d - 1], ys[d - 1]) for d in range(1, NY)
+    ]
 
     for copy in down_x:
         copy.wait_recv()
@@ -404,30 +454,66 @@
         send(DOWN_Z + d - 1, dz_send.at[(z + d) % NZ], dz_recv.at[d - 1], zs[d - 1]) for d in range(1, NZ)
     ]
 
-    for i in (1, 0, 2):
-        for copy in conv_z[i]:
-            copy.wait_recv()
-        total = cz_send[pl.ds(i, 1), pl.ds(z, 1)].reshape(16, 384).astype(F32)
-        for d in range(7):
-            total = total + cz_recv[i, d].astype(F32)
-        last_send[:, 384 * i : 384 * i + 384] = total.astype(BF)
+    for copy in conv_zy:
+        copy.wait_recv()
+    total = czy_send[pl.ds(y, 1)].reshape(2, 16, 384).astype(F32)
+    for d in range(3):
+        total = total + czy_recv[d].astype(F32)
+    last_sum[pl.ds(pair, 1), :, 768:] = total[0:1]
+    last_sum[pl.ds(1 - pair, 1), :, 768:] = total[1:2]
+    for copy in conv_yz:
+        copy.wait_recv()
+    halves = [cyz_send[pl.ds(z, 1)].astype(F32), 0.0]
+    for d in range(1, NZ):
+        halves[d % 2] = halves[d % 2] + cyz_recv[d - 1 : d].astype(F32)
+    last_sum[pl.ds(pair, 1), :, :768] = halves[0]
+    last_sum[pl.ds(1 - pair, 1), :, :768] = halves[1]
+    for h in range(2):
+        whole = last_sum[h]
+        for q in range(2):
+            pieces = [whole[:, 128 * s + 64 * q : 128 * s + 64 * q + 64] for s in range(9)]
+            last_send[h, q] = jnp.concatenate(pieces + [jnp.zeros((16, 64), F32)], axis=1).astype(BF)
+
+    def last(slot, h, q, to, sent_by=None):
+        return pltpu.make_async_remote_copy(
+            src_ref=last_send.at[h, q],
+            dst_ref=last_recv.at[slot],
+            send_sem=send_sem.at[CONV_LAST + (slot if sent_by is None else sent_by)],
+            recv_sem=recv_sem.at[CONV_LAST + slot],
+            device_id=to,
+            device_id_type=MESH,
+        )
+
+    near_l, far_l = 2 * l, 2 - 2 * l
+
     @pl.when(xh == c)
     def _():
-        copy = remote(CONV_LAST + 2, last_send, last_recv.at[2], (w, other_c))
-        copy.start()
-        remote(CONV_LAST, last_send, last_recv.at[0], (across, n)).wait_recv()
-        copy.wait_send()
+        copies = [
+            last(1, 1 - l, 0, (w, far_l)),
+            last(1, 1 - l, 1, (w, far_l + 1), 4),
+            last(0, l, 1 - c, (w, other_c)),
+        ]
+        for copy in copies:
+            copy.start()
+        for copy in copies:
+            copy.wait_send()
 
     @pl.when(xh != c)
     def _():
-        one = remote(CONV_LAST, last_send, last_recv.at[0], (across, n))
-        two = remote(CONV_LAST + 1, last_send, last_recv.at[1], (across, other_c))
-        one.start()
-        two.start()
-        two.wait_recv()
-        remote(CONV_LAST + 2, last_send, last_recv.at[2], (w, other_c)).wait_recv()
-        one.wait_send()
-        two.wait_send()
+        copies = [
+            last(2, l, 0, (across, near_l)),
+            last(2, l, 1, (across, near_l + 1), 4),
+            last(3, 1 - l, 0, (across, far_l)),
+            last(3, 1 - l, 1, (across, far_l + 1), 5),
+        ]
+        for copy in copies:
+            copy.start()
+        for copy in copies:
+            copy.wait_send()
+        last(0, l, c, (w, other_c)).wait_recv()
+
+    for slot in range(1, 4):
+        last(slot, l, c, (w, other_c)).wait_recv()
 
     for copy in down_z:
         copy.wait_recv()
@@ -437,13 +523,14 @@
     dl_send[...] = total
     down_last = send(DOWN_LAST, dl_send, dl_recv, (w, other_c))
 
-    one = jnp.where(c == xh, last_send[...], last_recv[2])
-    two = jnp.where(c == xh, last_recv[0], last_recv[1])
-    conv = (one.astype(F32) + two.astype(F32)) * factor
+    own = last_send[pl.ds(l, 1), pl.ds(c, 1)].reshape(16, 640)
+    conv = jnp.where(c == xh, own, last_recv[0]).astype(F32)
+    for slot in range(1, 4):
+        conv = conv + last_recv[slot].astype(F32)
+    conv = conv * factor
     for s in range(9):
-        own = jnp.where(c == 0, conv[:, 128 * s : 128 * s + 64], conv[:, 128 * s + 64 : 128 * s + 128])
         for k in range(3):
-            cg_out[3 * s + k] = own[4 * k : 4 * k + 4]
+            cg_out[3 * s + k] = conv[4 * k : 4 * k + 4, 64 * s : 64 * s + 64]
     down_last.wait_recv()
     theirs = dl_recv[...]
     both = jnp.concatenate([jnp.where(c == 0, total, theirs), jnp.where(c == 0, theirs, total)], axis=1)
@@ -480,21 +567,27 @@
         ((1024, 256), BF),
         ((2, 3, 10, 32, 128), BF),
         ((2, 3, 10, 32, 128), BF),
-        ((3, 34, 32, 128), BF),
+        ((3, 2, 18, 32, 128), BF),
         ((2, 128, 256), BF),
         ((4, 128, 256), BF),
+        ((384, 1024), BF),
         ((384, 1024), BF),
         ((3, 256, 256), F32),
         ((4, 128, 128), BF),
         ((4, 128, 128), BF),
         ((4, 128, 128), BF),
         ((4, 128, 128), BF),
-        ((3, 4, 3, 32, 384), BF),
-        ((3, 3, 3, 32, 384), BF),
-        ((3, 32, 384), F32),
-        ((8, 16, 384), F32),
-        ((3, 8, 16, 384), BF),
-        ((3, 7, 16, 384), BF),
+        ((4, 3, 32, 768), BF),
+        ((3, 3, 32, 768), BF),
+        ((3, 32, 768), F32),
+        ((8, 16, 768), F32),
+        ((8, 16, 768), BF),
+        ((7, 16, 768), BF),
+        ((8, 3, 16, 384), BF),
+        ((7, 3, 16, 384), BF),
+        ((4, 2, 16, 384), F32),
+        ((4, 2, 16, 384), BF),
+        ((3, 2, 16, 384), BF),
         ((1024, 128), BF),
         ((1024, 128), BF),
         ((2, 2, 16, 16, 128), F32),
@@ -506,8 +599,9 @@
         ((7, 8, 128), F32),
         ((8, 128), F32),
         ((8, 128), F32),
-        ((16, 1152), BF),
-        ((3, 16, 1152), BF),
+        ((2, 16, 1152), F32),
+        ((2, 2, 16, 640), BF),
+        ((4, 16, 640), BF),
     ]
     results = pl.pallas_call(
         functools.partial(kernel, factor),

time: 59.1 us -> 54.3 us (0.919)
  Pallas kernels: 58.4 us -> 53.6 us
    pallas_call x1, Pallas kernels: 56.3 us -> 51.5 us  [on_device(): pl.pallas_call(functools.partial(kernel, factor), name='unet_level', out_...]
where the time goes in v3:
time: 54.3 us; the launch traced here: 54.2 us
  Pallas kernels  53.6 us (99%)
  between operations  0.64 us (1%)
    pallas_call x1, Pallas kernels, on_device(): pl.pallas_call(functools.partial(kernel, factor), name='unet_level', out_...  51.5 us
    pallas_call x1, Pallas kernels, on_device(): pl.pallas_call(write_out, name='write_out', out_shape=tuple((jax.ShapeDty...  2.03 us

profile of v3, /device:TPU:1, one launch (start us, length us, event | category | flops | bytes accessed | tf_op | source)
XLA Modules:
  0.0 54.2 jit_solution(3763271197248766427)
XLA Ops:
  0.6 51.5 %unet_level.1 = (bf16[1024,64]{1,0:T(8,128)(2,1)}, bf16[2,8,2,64,128]{4,3,2,1,0:T(8,128)(2,1)}, f32[4,256]{1,0:T(4,128)}, f32[27,4,64]{2,1,0:T(4,128)}) custom-call(bf16[2,8,2,64,128]{4,3,2,1,0:T(8,128)(2,1)} %bitcast.5, bf16[1024,256]{1,0:T(8,128)(2,1)} %dw_ref.1, bf16[27,256,256]{2,1,0:T(8,128)(2,1)} %cw_ref.1, bf16[4,256,64]{2,1,0:T(8,128)(2,1)} %bitcast.7), custom_call_target="tpu_custom_call" | custom-call | flops 3200000000 | bytes 8000000 | tf_op jit(solution)/shard_map/unet_level/pallas_call | solution.py:606
  52.2 2.0 %write_out.1 = (bf16[1024,64]{1,0:T(8,128)(2,1)}, bf16[2,8,2,64,128]{4,3,2,1,0:T(8,128)(2,1)}, f32[4,256]{1,0:T(4,128)}, f32[27,4,64]{2,1,0:T(4,128)}) custom-call(bf16[1024,64]{1,0:T(8,128)(2,1)} %get-tuple-element.12.refs_0_, bf16[2,8,2,64,128]{4,3,2,1,0:T(8,128)(2,1)} %get-tuple-element.13.refs_1_, f32[4,256]{1,0:T(4,128)} %get-tuple-element.14.refs_2_, ...), custom_call_target="tpu_custom_call" | custom-call | tf_op jit(solution)/shard_map/write_out/pallas_call | solution.py:633

commit v4 on v3

v4 whole, which is shorter than its diff:
```python
import functools
import math

import jax
import jax.numpy as jnp
from jax import lax
from jax.experimental import pallas as pl
from jax.experimental.pallas import tpu as pltpu
from jax.sharding import PartitionSpec as P

MESH = pl.DeviceIdType.MESH
BF = jnp.bfloat16
F32 = jnp.float32
Y_TAPS = ((0, 0), (0, 1), (0, 2), (1, 0), (1, 1), (1, 2))
Z_TAPS = ((2, 0), (2, 1), (2, 2))
YL, ZL = 128 * len(Y_TAPS), 128 * len(Z_TAPS)
NY, NZ = 4, 8

COT, DEEP_ROWS, DEEP_LOW, DEEP_HIGH, DEEP_OWN, DEEP_OUTER, DEEP_CORE, ACT = range(8)
GRAD_ROWS, GRAD_LOW, GRAD_HIGH, GRAD_SHARE, CONV_Y, CONV_YZ, CONV_Z, CONV_ZY = range(8, 16)
DOWN_C, DOWN_XY, DOWN_Z, DOWN_LAST, CONV_LAST, CONV_CORE = range(16, 22)
GROUPS = 22
Y_BLOCKS, Z_BLOCKS = -(-3 * len(Y_TAPS) // 4), -(-3 * len(Z_TAPS) // 4)


def matmul(a, b):
    return jnp.dot(a, b, preferred_element_type=F32)


def matmul_nt(a, b):
    return lax.dot_general(a, b, (((1,), (1,)), ((), ())), preferred_element_type=F32)


def kernel(
    factor,
    vol_ref,
    dw_ref,
    cw_ref,
    cot_ref,
    act_out,
    vg_out,
    dg_out,
    cg_out,
    vol,
    dw,
    cw,
    cot,
    wide_f32,
    patches,
    patches_t,
    deep,
    grad,
    deep_all,
    grad_t_send,
    grad_t,
    grad_rows,
    grad_rows_z,
    acc,
    cot_send,
    cot_recv,
    act_send,
    act_recv,
    act_vmem,
    cy_send,
    cy_recv,
    sum_rows,
    cyz_rows,
    cyz_send,
    cyz_recv,
    cz_send,
    cz_recv,
    czy_rows,
    czy_send,
    czy_recv,
    dc_send,
    dc_recv,
    dx_rows,
    dx_send,
    dx_recv,
    dz_send,
    dz_recv,
    dl_send,
    dl_recv,
    cg_vmem,
    dg_vmem,
    last_sum,
    last_send,
    last_recv,
    local_sem,
    send_sem,
    recv_sem,
):
    w = lax.axis_index("wide")
    n = lax.axis_index("narrow")
    y, z, xh = w // 16, (w // 2) % NZ, w % 2
    l, c = n // 2, n % 2
    pair = z % 2

    def wide_of(yy, zz, xx):
        return ((yy % NY) * NZ + zz % NZ) * 2 + xx

    near = [(w, (n + d) % 4) for d in range(1, 4)]
    up, down = (w + 1) % 64, (w + 63) % 64
    right, left = (n + 1) % 4, (n + 3) % 4
    depth = [(s, (n + d) % 4) for s in (up, down) for d in range(4)]
    ys = [(wide_of(y + d, z, xh), n) for d in range(1, NY)]
    zs = [(wide_of(y, z + d, xh), n) for d in range(1, NZ)]
    other_c = n + 1 - 2 * c
    across = wide_of(y, z, 1 - xh)
    other_l = (n + 2) % 4
    beside = wide_of(y, z + 1 - 2 * pair, xh)
    xys = [
        (dy, dx, dl, (wide_of(y + dy, z, (xh + dx) % 2), n + 2 * dl * (1 - 2 * l)))
        for dy in range(NY)
        for dx in range(2)
        for dl in range(2)
        if dy or dx or dl
    ]

    barrier = pltpu.get_barrier_semaphore()
    partners = near + depth + ys + zs + [to for dy, dx, dl, to in xys if dy and (dx or dl)]
    for who in partners:
        pl.semaphore_signal(barrier, inc=1, device_id=who, device_id_type=MESH)

    def remote(number, src, dst, who, received=None):
        return pltpu.make_async_remote_copy(
            src_ref=src,
            dst_ref=dst,
            send_sem=send_sem.at[number],
            recv_sem=recv_sem.at[number if received is None else received],
            device_id=who,
            device_id_type=MESH,
        )

    def send(*args, **kwargs):
        remote(*args, **kwargs).start()

    def arrived(number, ref):
        remote(number, ref, ref, near[0]).wait_recv()

    outgoing = []

    def sent(number, ref):
        outgoing.append(remote(number, ref, ref, near[0]))

    loads = [
        pltpu.make_async_copy(src, dst, local_sem.at[s])
        for s, (src, dst) in enumerate(((vol_ref, vol), (dw_ref, dw), (cot_ref, cot), (cw_ref, cw)))
    ]
    for copy in loads:
        copy.start()

    def send_halos(buf, base):
        def rows(to, plane, received):
            for who, first, at in ((right, 8, 0), (left, 1, 9)):
                src = buf.at[:, 1, pl.ds(first, 1)]
                send(base, src, buf.at[:, plane, pl.ds(at, 1)], (to, who), received=received)

        rows(w, 1, base)
        for s, (to, plane) in enumerate(((up, 0), (down, 2))):
            planes = buf.at[:, plane, pl.ds(1, 8)]
            send(base + 1, buf.at[:, 1, pl.ds(1, 8)], planes, (to, n), received=base + 1 + s)
            rows(to, plane, base + 1 + s)
        sent(base, buf.at[:, 1, pl.ds(0, 6)])
        sent(base + 1, buf.at[:, pl.ds(0, 2), pl.ds(0, 8)])

    def clear_rows(buf, plane):
        @pl.when(n == 0)
        def _():
            buf[:, plane, 0:1] = jnp.zeros((2, 1, 32, 128), BF)

        @pl.when(n == 3)
        def _():
            buf[:, plane, 9:10] = jnp.zeros((2, 1, 32, 128), BF)

    def rows_arrive(buf, base):
        arrived(base, buf.at[:, 1, pl.ds(0, 2)])
        clear_rows(buf, 1)

    def plane_arrives(buf, base, plane):
        arrived(base + 1 + plane // 2, buf.at[:, plane])
        clear_rows(buf, plane)

        @pl.when(w == (0 if plane == 0 else 63))
        def _():
            buf[:, plane] = jnp.zeros((2, 10, 32, 128), BF)

    loads[0].wait()
    wide_f32[...] = vol[...].astype(F32)
    for a in range(2):
        for b in range(2):
            for e in range(2):
                part = wide_f32[a, :, b, pl.ds(e, 32, stride=2), :].reshape(256, 128).astype(BF)
                at = (4 * a + 2 * b + e) * 128
                patches[:, at : at + 128] = part
    loads[1].wait()
    cells = matmul(patches[...], dw[...]).astype(BF)
    for half in range(2):
        deep[half, 1, 1:9] = cells[:, 128 * half : 128 * half + 128].reshape(8, 32, 128)

    from_rows, to_rows = pl.ds(c, 9), pl.ds(9 * c, 9)
    outer, inner = 2 * pair, 2 - 2 * pair

    def to_core(src, plane, chip):
        send(DEEP_CORE, src, deep_all.at[plane, chip, to_rows], (w, other_c))

    def share_core(plane):
        deep_all[plane, pl.ds(pair, 1), to_rows] = deep[pl.ds(pair, 1), plane, from_rows]
        to_core(deep.at[pair, plane, from_rows], plane, pair)

    def share_across(plane, received):
        src = deep.at[1 - pair, plane, from_rows]
        send(DEEP_OWN, src, deep_all.at[plane, pair, to_rows], (beside, n), received=received)

    def pass_on(plane, received):
        theirs = deep_all.at[plane, 1 - pair, to_rows]
        arrived(received, theirs)
        to_core(theirs, plane, 1 - pair)

    pl.semaphore_wait(barrier, len(partners))
    send_halos(deep, DEEP_ROWS)
    loads[2].wait()
    for m in range(4):
        cot_send[m] = jnp.concatenate([cot[m, :128], cot[m, 128:]], axis=1)
    cot_recv[pl.ds(n, 1)] = cot_send[pl.ds(n, 1)]
    for d in range(1, 4):
        send(COT, cot_send.at[(n + d) % 4], cot_recv.at[n], near[d - 1])
    sent(COT, cot_send.at[pl.ds(0, 3)])
    cyz_rows[...] = jnp.zeros_like(cyz_rows)
    czy_rows[...] = jnp.zeros_like(czy_rows)

    for s in range(4):
        block = patches[:, 256 * s : 256 * s + 256].astype(F32)
        patches_t[256 * s : 256 * s + 256, :] = block.T.astype(BF)

    def window(buf, plane, first):
        return [buf[half, plane, first : first + 8].reshape(256, 128) for half in range(2)]

    def shifted(value, by, masked):
        column = lax.broadcasted_iota(jnp.int32, value.shape, 0) % 32
        return jnp.where(column == masked, 0.0, pltpu.roll(value, by, 0))

    loads[3].wait()
    for i in (1, 0, 2):
        if i == 1:
            rows_arrive(deep, DEEP_ROWS)
        else:
            plane_arrives(deep, DEEP_ROWS, i)
        share_core(i)
        if i == 1:
            share_across(1, DEEP_OWN)
        else:

            @pl.when(outer == i)
            def _():
                share_across(i, DEEP_OUTER)

        slab = jnp.concatenate(window(deep, i, 0) + window(deep, i, 1) + window(deep, i, 2), axis=1)
        for k in range(3):
            weights = jnp.concatenate([cw[9 * i + 3 * j + k] for j in range(3)], axis=0)
            term = matmul(slab, weights)
            acc[k] = term if i == 1 else acc[k] + term
    deep_all[pl.ds(outer, 1), pl.ds(1 - pair, 1), to_rows] = deep[pl.ds(pair, 1), pl.ds(inner, 1), from_rows]
    to_core(deep.at[pair, inner, from_rows], outer, 1 - pair)
    sent(DEEP_OWN, deep.at[:, 1, pl.ds(0, 9)])
    preact = shifted(acc[0], 1, 0) + acc[1] + shifted(acc[2], 255, 31)

    arrived(COT, cot_recv.at[pl.ds(0, 3)])
    cotangent = jnp.concatenate(
        [
            jnp.concatenate([cot_recv[m][:, :64], cot_recv[m][:, 64:]], axis=0)
            for m in range(4)
        ],
        axis=1,
    ).astype(F32)
    sigma = 1.0 / (1.0 + jnp.exp(-preact))
    activated = (preact * sigma).astype(BF)
    grad_pre = (cotangent * (sigma * (1.0 + preact * (1.0 - sigma)))).astype(BF)
    for half in range(2):
        grad[half, 1, 1:9] = grad_pre[:, 128 * half : 128 * half + 128].reshape(8, 32, 128)

    row = lax.broadcasted_iota(jnp.int32, (256, 256), 0)
    column = lax.broadcasted_iota(jnp.int32, (256, 256), 1)
    q = row % 128
    source = (q // 32) * 64 + ((q // 4) % 8) * 8 + (row // 128) * 4 + q % 4
    order = jnp.where(column == source, 1.0, 0.0).astype(BF)
    turned = matmul_nt(order, grad_pre).astype(BF)
    grad_t_send[0] = turned[:128]
    grad_t_send[1] = turned[128:]
    slot = 2 * pair + c
    grad_t[pl.ds(slot, 1)] = grad_t_send[pl.ds(c, 1)]
    mine = grad_t.at[slot]
    send(GRAD_SHARE, grad_t_send.at[1 - c], mine, (beside, other_c))
    send(GRAD_SHARE, grad_t_send.at[c], mine, (beside, n))
    send(GRAD_SHARE, grad_t_send.at[1 - c], mine, (w, other_c))
    sent(GRAD_SHARE, grad_t.at[pl.ds(0, 3)])
    send_halos(grad, GRAD_ROWS)

    pass_on(1, DEEP_OWN)
    pass_on(inner, DEEP_OUTER)
    sent(DEEP_CORE, deep_all.at[:, :, pl.ds(0, 9)])

    arrived(GRAD_SHARE, grad_t.at[pl.ds(0, 3)])
    lane = lax.broadcasted_iota(jnp.int32, (128, 256), 1) % 32
    for m in range(4):
        block = grad_t[m].astype(F32)
        at = 256 * m
        grad_rows[0:128, at : at + 256] = jnp.where(lane == 31, 0.0, pltpu.roll(block, 255, 1)).astype(BF)
        grad_rows[128:256, at : at + 256] = grad_t[m]
        grad_rows[256:384, at : at + 256] = jnp.where(lane == 0, 0.0, pltpu.roll(block, 1, 1)).astype(BF)
    def cells_at(i, j):
        return jnp.concatenate([deep_all[i, s, j : j + 16].reshape(512, 128) for s in range(2)], axis=0)

    arrived(DEEP_CORE, deep_all.at[:, :, pl.ds(0, 9)])
    slab = jnp.concatenate([cells_at(i, j) for i, j in Y_TAPS], axis=1)
    term = matmul(grad_rows[...], slab).astype(BF)
    for yy in range(NY):
        for k in range(3):
            at = 128 * k + 32 * yy
            cy_send[yy, k] = term[at : at + 32]
    for d in range(1, NY):
        send(CONV_Y, cy_send.at[(y + d) % NY], cy_recv.at[d - 1], ys[d - 1])
    sent(CONV_Y, cy_recv)
    row = lax.broadcasted_iota(jnp.int32, (128, 128), 0)
    column = lax.broadcasted_iota(jnp.int32, (128, 128), 1)
    source = ((row // 4) % 4) * 32 + (row // 16) * 4 + row % 4
    order = jnp.where(column == source, 1.0, 0.0).astype(BF)
    for k in range(3):
        grad_rows_z[128 * k : 128 * k + 128, :] = matmul(order, grad_rows[128 * k : 128 * k + 128, :]).astype(BF)
    slab = jnp.concatenate([cells_at(i, j) for i, j in Z_TAPS], axis=1)
    term = matmul(grad_rows_z[...], slab).astype(BF)
    for zz in range(NZ):
        for k in range(3):
            at = 128 * k + 16 * zz
            cz_send[zz, k] = term[at : at + 16]
    for d in range(1, NZ):
        send(CONV_Z, cz_send.at[(z + d) % NZ], cz_recv.at[d - 1], zs[d - 1])
    sent(CONV_Z, cz_recv)

    for i in (1, 2, 0):
        plane = 2 - i
        if i == 1:
            rows_arrive(grad, GRAD_ROWS)
        else:
            plane_arrives(grad, GRAD_ROWS, plane)
        slab = jnp.concatenate(
            window(grad, plane, 2) + window(grad, plane, 1) + window(grad, plane, 0), axis=1
        )
        for k in range(3):
            weights = jnp.concatenate([cw[9 * i + 3 * j + k] for j in range(3)], axis=1)
            term = matmul_nt(slab, weights)
            acc[k] = term if i == 1 else acc[k] + term
    grad_deep = (shifted(acc[0], 255, 31) + acc[1] + shifted(acc[2], 1, 0)).astype(BF)

    partial = matmul(patches_t[...], grad_deep)
    low, high = partial[:, :128], partial[:, 128:]
    dc_send[...] = jnp.where(c == 0, high, low).astype(BF)
    send(DOWN_C, dc_send, dc_recv, (w, other_c))
    sent(DOWN_C, dc_send)
    kept = jnp.where(c == 0, low, high)

    for m in range(4):
        part = activated[:, 64 * m : 64 * m + 64]
        act_send[m] = jnp.concatenate([part[:128], part[128:]], axis=1)
    act_recv[pl.ds(n, 1)] = act_send[pl.ds(n, 1)]
    for d in range(1, 4):
        send(ACT, act_send.at[(n + d) % 4], act_recv.at[n], near[d - 1])
    sent(ACT, act_send.at[pl.ds(0, 3)])

    spread = matmul_nt(grad_deep, dw[...])
    for a in range(2):
        for b in range(2):
            for e in range(2):
                at = (4 * a + 2 * b + e) * 128
                wide_f32[a, :, b, pl.ds(e, 32, stride=2), :] = spread[:, at : at + 128].reshape(8, 32, 128)
    vol[...] = wide_f32[...].astype(BF)
    vg_write = pltpu.make_async_copy(vol, vg_out, local_sem.at[0])
    vg_write.start()

    arrived(DOWN_C, dc_recv)
    total = (kept + dc_recv[...].astype(F32)).reshape(16, 2, 2, 2, 8, 128)
    for xx in range(2):
        for ll in range(2):
            for zz in range(2):
                dx_rows[xx, ll, :, 8 * zz : 8 * zz + 8] = total[:, zz, xx, ll]
    dx_send[...] = dx_rows[...].astype(BF)
    for s, (dy, dx, dl, to) in enumerate(xys):
        src = dx_send.at[(xh + dx) % 2, (l + dl) % 2, pl.ds(4 * ((y + dy) % NY), 4)]
        send(DOWN_XY, src, dx_recv.at[s], to)
    sent(DOWN_XY, dx_recv)

    arrived(CONV_Y, cy_recv)
    total = cy_send[pl.ds(y, 1)].reshape(3, 32, YL).astype(F32)
    for d in range(3):
        total = total + cy_recv[d].astype(F32)
    sum_rows[...] = total
    for zz in range(NZ):
        for m in range(3 * len(Y_TAPS)):
            part = sum_rows[m % 3, 4 * zz : 4 * zz + 4, 128 * (m // 3) : 128 * (m // 3) + 128]
            cyz_rows[zz, 4 * (m % 4) : 4 * (m % 4) + 4, 128 * (m // 4) : 128 * (m // 4) + 128] = part
    cyz_send[...] = cyz_rows[...].astype(BF)
    for d in range(1, NZ):
        send(CONV_YZ, cyz_send.at[(z + d) % NZ], cyz_recv.at[d - 1], zs[d - 1])
    sent(CONV_YZ, cyz_recv)

    arrived(CONV_Z, cz_recv)
    halves = [cz_send[pl.ds(z, 1)].reshape(3, 16, ZL).astype(F32), 0.0]
    for d in range(1, NZ):
        halves[d % 2] = halves[d % 2] + cz_recv[d - 1].astype(F32)
    for h in range(2):
        sum_rows[:, :16, :ZL] = halves[h]
        for yy in range(NY):
            for m in range(3 * len(Z_TAPS)):
                part = sum_rows[m % 3, 4 * yy : 4 * yy + 4, 128 * (m // 3) : 128 * (m // 3) + 128]
                czy_rows[yy, h, 4 * (m % 4) : 4 * (m % 4) + 4, 128 * (m // 4) : 128 * (m // 4) + 128] = part
    czy_send[...] = czy_rows[...].astype(BF)
    for d in range(1, NY):
        send(CONV_ZY, czy_send.at[(y + d) % NY], czy_recv.at[d - 1], ys[d - 1])
    sent(CONV_ZY, czy_recv)

    arrived(DOWN_XY, dx_recv)
    total = dx_rows[pl.ds(xh, 1), pl.ds(l, 1), pl.ds(4 * y, 4)].reshape(4, 16, 128)
    for s in range(15):
        total = total + dx_recv[s].astype(F32)
    dz_send[...] = total.reshape(NZ, 8, 128)
    for d in range(1, NZ):
        send(DOWN_Z, dz_send.at[(z + d) % NZ], dz_recv.at[d - 1], zs[d - 1])
    sent(DOWN_Z, dz_recv)

    arrived(ACT, act_recv.at[pl.ds(0, 3)])
    for m in range(4):
        act_vmem[256 * m : 256 * m + 128] = act_recv[m][:, :64]
        act_vmem[256 * m + 128 : 256 * m + 256] = act_recv[m][:, 64:]
    act_write = pltpu.make_async_copy(act_vmem, act_out, local_sem.at[1])
    act_write.start()

    arrived(CONV_ZY, czy_recv)
    total = czy_send[pl.ds(y, 1)].reshape(2, 16, 128 * Z_BLOCKS).astype(F32)
    for d in range(3):
        total = total + czy_recv[d].astype(F32)
    last_sum[pl.ds(pair, 1), :, 128 * Y_BLOCKS :] = total[0:1]
    last_sum[pl.ds(1 - pair, 1), :, 128 * Y_BLOCKS :] = total[1:2]
    arrived(CONV_YZ, cyz_recv)
    halves = [cyz_send[pl.ds(z, 1)].astype(F32), 0.0]
    for d in range(1, NZ):
        halves[d % 2] = halves[d % 2] + cyz_recv[d - 1 : d].astype(F32)
    last_sum[pl.ds(pair, 1), :, : 128 * Y_BLOCKS] = halves[0]
    last_sum[pl.ds(1 - pair, 1), :, : 128 * Y_BLOCKS] = halves[1]
    for h in range(2):
        whole = last_sum[h]
        for q in range(2):
            pieces = [whole[:, 128 * b + 64 * q : 128 * b + 64 * q + 64] for b in range(Y_BLOCKS + Z_BLOCKS)]
            last_send[h, q] = jnp.concatenate(pieces, axis=1).astype(BF)

    def last(slot, h, q, to):
        send(CONV_LAST, last_send.at[h, q], last_recv.at[slot], to, received=CONV_LAST if slot else CONV_CORE)

    near_l, far_l = 2 * l, 2 - 2 * l

    @pl.when(xh == c)
    def _():
        last(1, 1 - l, 0, (w, far_l))
        last(1, 1 - l, 1, (w, far_l + 1))
        last(0, l, 1 - c, (w, other_c))

    @pl.when(xh != c)
    def _():
        last(2, l, 0, (across, near_l))
        last(2, l, 1, (across, near_l + 1))
        last(3, 1 - l, 0, (across, far_l))
        last(3, 1 - l, 1, (across, far_l + 1))

    arrived(DOWN_Z, dz_recv)
    total = dz_send[pl.ds(z, 1)].reshape(8, 128)
    for d in range(7):
        total = total + dz_recv[d]
    dl_send[...] = total
    send(DOWN_LAST, dl_send, dl_recv, (w, other_c))
    sent(DOWN_LAST, dl_send)

    @pl.when(xh == c)
    def _():
        remote(CONV_LAST, last_recv.at[pl.ds(0, 3)], last_recv.at[pl.ds(0, 3)], near[0]).wait_send()

    @pl.when(xh != c)
    def _():
        remote(CONV_LAST, last_recv, last_recv, near[0]).wait_send()
        arrived(CONV_CORE, last_recv.at[0])

    arrived(CONV_LAST, last_recv.at[pl.ds(1, 3)])
    own = last_send[pl.ds(l, 1), pl.ds(c, 1)].reshape(16, 64 * (Y_BLOCKS + Z_BLOCKS))
    conv = jnp.where(c == xh, own, last_recv[0]).astype(F32)
    for slot in range(1, 4):
        conv = conv + last_recv[slot].astype(F32)
    conv = conv * factor
    for first, taps in ((0, Y_TAPS), (Y_BLOCKS, Z_TAPS)):
        for m in range(3 * len(taps)):
            i, j = taps[m // 3]
            at = 64 * (first + m // 4)
            cg_vmem[9 * i + 3 * j + m % 3] = conv[4 * (m % 4) : 4 * (m % 4) + 4, at : at + 64]
    cg_write = pltpu.make_async_copy(cg_vmem, cg_out, local_sem.at[2])
    cg_write.start()
    arrived(DOWN_LAST, dl_recv)
    theirs = dl_recv[...]
    both = jnp.concatenate([jnp.where(c == 0, total, theirs), jnp.where(c == 0, theirs, total)], axis=1)
    dg_vmem[...] = jnp.where(c == 0, both[:4], both[4:]) * factor
    dg_write = pltpu.make_async_copy(dg_vmem, dg_out, local_sem.at[3])
    dg_write.start()

    for copy in outgoing:
        copy.wait_send()
    for copy in (vg_write, act_write, cg_write, dg_write):
        copy.wait()


def write_out(*refs):
    arrays = (len(refs) - 1) // 2
    sems = refs[-1]
    copies = [
        pltpu.make_async_copy(src, dst, sems.at[s])
        for s, (src, dst) in enumerate(zip(refs[:arrays], refs[arrays:-1]))
    ]
    for copy in copies:
        copy.start()
    for copy in copies:
        copy.wait()


def on_device(volume, down_weight, conv_weight, cotangent):
    factor = 1.0 / (32 * math.sqrt(64))
    hbm = pl.BlockSpec(memory_space=pltpu.HBM)
    vmem = pl.BlockSpec(memory_space=pltpu.VMEM)
    scratch = [
        ((2, 8, 2, 64, 128), BF),
        ((1024, 256), BF),
        ((27, 256, 256), BF),
        ((4, 256, 64), BF),
        ((2, 8, 2, 64, 128), F32),
        ((256, 1024), BF),
        ((1024, 256), BF),
        ((2, 3, 10, 32, 128), BF),
        ((2, 3, 10, 32, 128), BF),
        ((3, 2, 18, 32, 128), BF),
        ((2, 128, 256), BF),
        ((4, 128, 256), BF),
        ((384, 1024), BF),
        ((384, 1024), BF),
        ((3, 256, 256), F32),
        ((4, 128, 128), BF),
        ((4, 128, 128), BF),
        ((4, 128, 128), BF),
        ((4, 128, 128), BF),
        ((1024, 64), BF),
        ((4, 3, 32, YL), BF),
        ((3, 3, 32, YL), BF),
        ((3, 32, YL), F32),
        ((8, 16, 128 * Y_BLOCKS), F32),
        ((8, 16, 128 * Y_BLOCKS), BF),
        ((7, 16, 128 * Y_BLOCKS), BF),
        ((8, 3, 16, ZL), BF),
        ((7, 3, 16, ZL), BF),
        ((4, 2, 16, 128 * Z_BLOCKS), F32),
        ((4, 2, 16, 128 * Z_BLOCKS), BF),
        ((3, 2, 16, 128 * Z_BLOCKS), BF),
        ((1024, 128), BF),
        ((1024, 128), BF),
        ((2, 2, 16, 16, 128), F32),
        ((2, 2, 16, 16, 128), BF),
        ((15, 4, 16, 128), BF),
        ((8, 8, 128), F32),
        ((7, 8, 128), F32),
        ((8, 128), F32),
        ((8, 128), F32),
        ((27, 4, 64), F32),
        ((4, 256), F32),
        ((2, 16, 128 * (Y_BLOCKS + Z_BLOCKS)), F32),
        ((2, 2, 16, 64 * (Y_BLOCKS + Z_BLOCKS)), BF),
        ((4, 16, 64 * (Y_BLOCKS + Z_BLOCKS)), BF),
    ]
    results = pl.pallas_call(
        functools.partial(kernel, factor),
        name="unet_level",
        out_shape=(
            jax.ShapeDtypeStruct((1024, 64), BF),
            jax.ShapeDtypeStruct((2, 8, 2, 64, 128), BF),
            jax.ShapeDtypeStruct((4, 256), F32),
            jax.ShapeDtypeStruct((27, 4, 64), F32),
        ),
        in_specs=[hbm] * 4,
        out_specs=(hbm,) * 4,
        scratch_shapes=[pltpu.VMEM(shape, dtype) for shape, dtype in scratch]
        + [
            pltpu.SemaphoreType.DMA((4,)),
            pltpu.SemaphoreType.DMA((GROUPS,)),
            pltpu.SemaphoreType.DMA((GROUPS,)),
        ],
        compiler_params=pltpu.CompilerParams(
            collective_id=0, has_side_effects=True, vmem_limit_bytes=56 * 1024 * 1024
        ),
        cost_estimate=pl.CostEstimate(flops=3200000000, bytes_accessed=8000000, transcendentals=65536),
    )(
        volume.reshape(2, 8, 2, 64, 128),
        down_weight,
        conv_weight,
        cotangent.reshape(4, 256, 64),
    )
    activated, volume_grad, down_grad, conv_grad = pl.pallas_call(
        write_out,
        name="write_out",
        out_shape=tuple(jax.ShapeDtypeStruct(r.shape, r.dtype) for r in results),
        in_specs=[vmem] * 4,
        out_specs=(hbm,) * 4,
        scratch_shapes=[pltpu.SemaphoreType.DMA((4,))],
    )(*results)
    return (
        activated.reshape(1, 32, 32, 64),
        volume_grad.reshape(2, 16, 64, 128),
        down_grad,
        conv_grad.transpose(0, 2, 1),
    )


def solution(mesh):
    placed = (P("wide", "narrow", None, None), P(), P(), P("wide", None, None, "narrow"))
    return jax.shard_map(
        on_device,
        mesh=mesh,
        in_specs=placed,
        out_specs=(
            P("wide", None, None, "narrow"),
            P("wide", "narrow", None, None),
            P(("wide", "narrow"), None),
            P(None, "narrow", "wide"),
        ),
        check_vma=False,
    )
```

time: 54.3 us -> 51.9 us (0.956)
  Pallas kernels: 53.6 us -> 51.1 us
    pallas_call x1, Pallas kernels: 51.5 us -> 49.1 us  [on_device(): pl.pallas_call(functools.partial(kernel, factor), name='unet_level', out_...]
where the time goes in v4:
time: 51.9 us; the launch traced here: 51.8 us
  Pallas kernels  51.1 us (98%)
  between operations  0.64 us (1%)
    pallas_call x1, Pallas kernels, on_device(): pl.pallas_call(functools.partial(kernel, factor), name='unet_level', out_...  49.1 us
    pallas_call x1, Pallas kernels, on_device(): pl.pallas_call(write_out, name='write_out', out_shape=tuple((jax.ShapeDty...  2.03 us

profile of v4, /device:TPU:1, one launch (start us, length us, event | category | flops | bytes accessed | tf_op | source)
XLA Modules:
  0.0 51.8 jit_solution(7474529521407529142)
XLA Ops:
  0.6 49.1 %unet_level.1 = (bf16[1024,64]{1,0:T(8,128)(2,1)}, bf16[2,8,2,64,128]{4,3,2,1,0:T(8,128)(2,1)}, f32[4,256]{1,0:T(4,128)}, f32[27,4,64]{2,1,0:T(4,128)}) custom-call(bf16[2,8,2,64,128]{4,3,2,1,0:T(8,128)(2,1)} %bitcast.5, bf16[1024,256]{1,0:T(8,128)(2,1)} %dw_ref.1, bf16[27,256,256]{2,1,0:T(8,128)(2,1)} %cw_ref.1, bf16[4,256,64]{2,1,0:T(8,128)(2,1)} %bitcast.7), custom_call_target="tpu_custom_call" | custom-call | flops 3200000000 | bytes 8000000 | tf_op jit(solution)/shard_map/unet_level/pallas_call | solution.py:580
  49.7 2.0 %write_out.1 = (bf16[1024,64]{1,0:T(8,128)(2,1)}, bf16[2,8,2,64,128]{4,3,2,1,0:T(8,128)(2,1)}, f32[4,256]{1,0:T(4,128)}, f32[27,4,64]{2,1,0:T(4,128)}) custom-call(bf16[1024,64]{1,0:T(8,128)(2,1)} %get-tuple-element.12.refs_0_, bf16[2,8,2,64,128]{4,3,2,1,0:T(8,128)(2,1)} %get-tuple-element.13.refs_1_, f32[4,256]{1,0:T(4,128)} %get-tuple-element.14.refs_2_, ...), custom_call_target="tpu_custom_call" | custom-call | tf_op jit(solution)/shard_map/write_out/pallas_call | solution.py:607

commit v5 on v4

--- a/solution.py
+++ b/solution.py
@@ -15,6 +15,7 @@
 Z_TAPS = ((2, 0), (2, 1), (2, 2))
 YL, ZL = 128 * len(Y_TAPS), 128 * len(Z_TAPS)
 NY, NZ = 4, 8
+Y_ORDER, Z_ORDER = (2, 1, 3), (4, 3, 5, 2, 6, 1, 7)
 
 COT, DEEP_ROWS, DEEP_LOW, DEEP_HIGH, DEEP_OWN, DEEP_OUTER, DEEP_CORE, ACT = range(8)
 GRAD_ROWS, GRAD_LOW, GRAD_HIGH, GRAD_SHARE, CONV_Y, CONV_YZ, CONV_Z, CONV_ZY = range(8, 16)
@@ -135,13 +136,32 @@
     def send(*args, **kwargs):
         remote(*args, **kwargs).start()
 
-    def arrived(number, ref):
-        remote(number, ref, ref, near[0]).wait_recv()
+    def finish(number, ref, edge_ref, receiving):
+        def wait(ref):
+            copy = remote(number, ref, ref, near[0])
+            if receiving:
+                copy.wait_recv()
+            else:
+                copy.wait_send()
+
+        if edge_ref is None:
+            wait(ref)
+        else:
+            pl.when(inside)(lambda: wait(ref))
+            pl.when(jnp.logical_not(inside))(lambda: wait(edge_ref))
+
+    def arrived(number, ref, edge_ref=None):
+        finish(number, ref, edge_ref, True)
 
     outgoing = []
 
-    def sent(number, ref):
-        outgoing.append(remote(number, ref, ref, near[0]))
+    def sent(number, ref, edge_ref=None):
+        outgoing.append((number, ref, edge_ref))
+
+    def flush(numbers):
+        for group in [group for group in outgoing if group[0] in numbers]:
+            finish(*group, False)
+            outgoing.remove(group)
 
     loads = [
         pltpu.make_async_copy(src, dst, local_sem.at[s])
@@ -150,18 +170,25 @@
     for copy in loads:
         copy.start()
 
+    inside = (n == 1) | (n == 2)
+    far = (w + 63 + 2 * xh) % 64
+
     def send_halos(buf, base):
         def rows(to, plane, received):
-            for who, first, at in ((right, 8, 0), (left, 1, 9)):
-                src = buf.at[:, 1, pl.ds(first, 1)]
-                send(base, src, buf.at[:, plane, pl.ds(at, 1)], (to, who), received=received)
+            for missing, who, first, at in ((3, n + 1, 8, 0), (0, n - 1, 1, 9)):
+
+                @pl.when(n != missing)
+                def _():
+                    src = buf.at[:, 1, pl.ds(first, 1)]
+                    send(base, src, buf.at[:, plane, pl.ds(at, 1)], (to, who), received=received)
 
         rows(w, 1, base)
-        for s, (to, plane) in enumerate(((up, 0), (down, 2))):
-            planes = buf.at[:, plane, pl.ds(1, 8)]
+        for to, s in ((far, 1 - xh), (across, xh)):
+            rows(to, 2 * s, base + 1 + s)
+        for to, s in ((far, 1 - xh), (across, xh)):
+            planes = buf.at[:, 2 * s, pl.ds(1, 8)]
             send(base + 1, buf.at[:, 1, pl.ds(1, 8)], planes, (to, n), received=base + 1 + s)
-            rows(to, plane, base + 1 + s)
-        sent(base, buf.at[:, 1, pl.ds(0, 6)])
+        sent(base, buf.at[:, 1, pl.ds(0, 6)], buf.at[:, 1, pl.ds(0, 3)])
         sent(base + 1, buf.at[:, pl.ds(0, 2), pl.ds(0, 8)])
 
     def clear_rows(buf, plane):
@@ -174,11 +201,11 @@
             buf[:, plane, 9:10] = jnp.zeros((2, 1, 32, 128), BF)
 
     def rows_arrive(buf, base):
-        arrived(base, buf.at[:, 1, pl.ds(0, 2)])
+        arrived(base, buf.at[:, 1, pl.ds(0, 2)], buf.at[:, 1, pl.ds(0, 1)])
         clear_rows(buf, 1)
 
     def plane_arrives(buf, base, plane):
-        arrived(base + 1 + plane // 2, buf.at[:, plane])
+        arrived(base + 1 + plane // 2, buf.at[:, plane], buf.at[:, plane, pl.ds(0, 9)])
         clear_rows(buf, plane)
 
         @pl.when(w == (0 if plane == 0 else 63))
@@ -282,7 +309,7 @@
     row = lax.broadcasted_iota(jnp.int32, (256, 256), 0)
     column = lax.broadcasted_iota(jnp.int32, (256, 256), 1)
     q = row % 128
-    source = (q // 32) * 64 + ((q // 4) % 8) * 8 + (row // 128) * 4 + q % 4
+    source = (q // 32) * 64 + ((q // 4) % 8) * 8 + (1 - row // 128) * 4 + q % 4
     order = jnp.where(column == source, 1.0, 0.0).astype(BF)
     turned = matmul_nt(order, grad_pre).astype(BF)
     grad_t_send[0] = turned[:128]
@@ -318,7 +345,7 @@
         for k in range(3):
             at = 128 * k + 32 * yy
             cy_send[yy, k] = term[at : at + 32]
-    for d in range(1, NY):
+    for d in Y_ORDER:
         send(CONV_Y, cy_send.at[(y + d) % NY], cy_recv.at[d - 1], ys[d - 1])
     sent(CONV_Y, cy_recv)
     row = lax.broadcasted_iota(jnp.int32, (128, 128), 0)
@@ -333,7 +360,8 @@
         for k in range(3):
             at = 128 * k + 16 * zz
             cz_send[zz, k] = term[at : at + 16]
-    for d in range(1, NZ):
+    flush((GRAD_ROWS, GRAD_LOW))
+    for d in Z_ORDER:
         send(CONV_Z, cz_send.at[(z + d) % NZ], cz_recv.at[d - 1], zs[d - 1])
     sent(CONV_Z, cz_recv)
 
@@ -399,7 +427,7 @@
             part = sum_rows[m % 3, 4 * zz : 4 * zz + 4, 128 * (m // 3) : 128 * (m // 3) + 128]
             cyz_rows[zz, 4 * (m % 4) : 4 * (m % 4) + 4, 128 * (m // 4) : 128 * (m // 4) + 128] = part
     cyz_send[...] = cyz_rows[...].astype(BF)
-    for d in range(1, NZ):
+    for d in Z_ORDER:
         send(CONV_YZ, cyz_send.at[(z + d) % NZ], cyz_recv.at[d - 1], zs[d - 1])
     sent(CONV_YZ, cyz_recv)
 
@@ -414,7 +442,7 @@
                 part = sum_rows[m % 3, 4 * yy : 4 * yy + 4, 128 * (m // 3) : 128 * (m // 3) + 128]
                 czy_rows[yy, h, 4 * (m % 4) : 4 * (m % 4) + 4, 128 * (m // 4) : 128 * (m // 4) + 128] = part
     czy_send[...] = czy_rows[...].astype(BF)
-    for d in range(1, NY):
+    for d in Y_ORDER:
         send(CONV_ZY, czy_send.at[(y + d) % NY], czy_recv.at[d - 1], ys[d - 1])
     sent(CONV_ZY, czy_recv)
 
@@ -423,7 +451,7 @@
     for s in range(15):
         total = total + dx_recv[s].astype(F32)
     dz_send[...] = total.reshape(NZ, 8, 128)
-    for d in range(1, NZ):
+    for d in Z_ORDER:
         send(DOWN_Z, dz_send.at[(z + d) % NZ], dz_recv.at[d - 1], zs[d - 1])
     sent(DOWN_Z, dz_recv)
 
@@ -457,13 +485,13 @@
 
     near_l, far_l = 2 * l, 2 - 2 * l
 
-    @pl.when(xh == c)
+    @pl.when(xh != c)
     def _():
         last(1, 1 - l, 0, (w, far_l))
         last(1, 1 - l, 1, (w, far_l + 1))
         last(0, l, 1 - c, (w, other_c))
 
-    @pl.when(xh != c)
+    @pl.when(xh == c)
     def _():
         last(2, l, 0, (across, near_l))
         last(2, l, 1, (across, near_l + 1))
@@ -478,18 +506,18 @@
     send(DOWN_LAST, dl_send, dl_recv, (w, other_c))
     sent(DOWN_LAST, dl_send)
 
-    @pl.when(xh == c)
+    @pl.when(xh != c)
     def _():
         remote(CONV_LAST, last_recv.at[pl.ds(0, 3)], last_recv.at[pl.ds(0, 3)], near[0]).wait_send()
 
-    @pl.when(xh != c)
+    @pl.when(xh == c)
     def _():
         remote(CONV_LAST, last_recv, last_recv, near[0]).wait_send()
         arrived(CONV_CORE, last_recv.at[0])
 
     arrived(CONV_LAST, last_recv.at[pl.ds(1, 3)])
     own = last_send[pl.ds(l, 1), pl.ds(c, 1)].reshape(16, 64 * (Y_BLOCKS + Z_BLOCKS))
-    conv = jnp.where(c == xh, own, last_recv[0]).astype(F32)
+    conv = jnp.where(c == xh, last_recv[0], own).astype(F32)
     for slot in range(1, 4):
         conv = conv + last_recv[slot].astype(F32)
     conv = conv * factor
@@ -507,8 +535,7 @@
     dg_write = pltpu.make_async_copy(dg_vmem, dg_out, local_sem.at[3])
     dg_write.start()
 
-    for copy in outgoing:
-        copy.wait_send()
+    flush(range(GROUPS))
     for copy in (vg_write, act_write, cg_write, dg_write):
         copy.wait()
 

time: 51.9 us -> 49.1 us (0.946)
  Pallas kernels: 51.1 us -> 48.4 us
    pallas_call x1, Pallas kernels: 49.1 us -> 46.4 us  [on_device(): pl.pallas_call(functools.partial(kernel, factor), name='unet_level', out_...]
where the time goes in v5:
time: 49.1 us; the launch traced here: 49 us
  Pallas kernels  48.4 us (99%)
  between operations  0.64 us (1%)
    pallas_call x1, Pallas kernels, on_device(): pl.pallas_call(functools.partial(kernel, factor), name='unet_level', out_...  46.4 us
    pallas_call x1, Pallas kernels, on_device(): pl.pallas_call(write_out, name='write_out', out_shape=tuple((jax.ShapeDty...  2.03 us

profile of v5, /device:TPU:1, one launch (start us, length us, event | category | flops | bytes accessed | tf_op | source)
XLA Modules:
  0.0 49.0 jit_solution(5135966411558783096)
XLA Ops:
  0.6 46.4 %unet_level.1 = (bf16[1024,64]{1,0:T(8,128)(2,1)}, bf16[2,8,2,64,128]{4,3,2,1,0:T(8,128)(2,1)}, f32[4,256]{1,0:T(4,128)}, f32[27,4,64]{2,1,0:T(4,128)}) custom-call(bf16[2,8,2,64,128]{4,3,2,1,0:T(8,128)(2,1)} %bitcast.5, bf16[1024,256]{1,0:T(8,128)(2,1)} %dw_ref.1, bf16[27,256,256]{2,1,0:T(8,128)(2,1)} %cw_ref.1, bf16[4,256,64]{2,1,0:T(8,128)(2,1)} %bitcast.7), custom_call_target="tpu_custom_call" | custom-call | flops 3200000000 | bytes 8000000 | tf_op jit(solution)/shard_map/unet_level/pallas_call | solution.py:607
  47.0 2.0 %write_out.1 = (bf16[1024,64]{1,0:T(8,128)(2,1)}, bf16[2,8,2,64,128]{4,3,2,1,0:T(8,128)(2,1)}, f32[4,256]{1,0:T(4,128)}, f32[27,4,64]{2,1,0:T(4,128)}) custom-call(bf16[1024,64]{1,0:T(8,128)(2,1)} %get-tuple-element.12.refs_0_, bf16[2,8,2,64,128]{4,3,2,1,0:T(8,128)(2,1)} %get-tuple-element.13.refs_1_, f32[4,256]{1,0:T(4,128)} %get-tuple-element.14.refs_2_, ...), custom_call_target="tpu_custom_call" | custom-call | tf_op jit(solution)/shard_map/write_out/pallas_call | solution.py:634

commit v6 on v5

--- a/solution.py
+++ b/solution.py
@@ -9,6 +9,7 @@
 from jax.sharding import PartitionSpec as P
 
 MESH = pl.DeviceIdType.MESH
+VMEM_BYTES = 55040 * 1024
 BF = jnp.bfloat16
 F32 = jnp.float32
 Y_TAPS = ((0, 0), (0, 1), (0, 2), (1, 0), (1, 1), (1, 2))
@@ -19,8 +20,8 @@
 
 COT, DEEP_ROWS, DEEP_LOW, DEEP_HIGH, DEEP_OWN, DEEP_OUTER, DEEP_CORE, ACT = range(8)
 GRAD_ROWS, GRAD_LOW, GRAD_HIGH, GRAD_SHARE, CONV_Y, CONV_YZ, CONV_Z, CONV_ZY = range(8, 16)
-DOWN_C, DOWN_XY, DOWN_Z, DOWN_LAST, CONV_LAST, CONV_CORE = range(16, 22)
-GROUPS = 22
+DOWN_C, DOWN_XY, DOWN_Z, CONV_LAST, CONV_CORE = range(16, 21)
+GROUPS = 21
 Y_BLOCKS, Z_BLOCKS = -(-3 * len(Y_TAPS) // 4), -(-3 * len(Z_TAPS) // 4)
 
 
@@ -51,6 +52,8 @@
     patches_t,
     deep,
     grad,
+    order,
+    order_z,
     deep_all,
     grad_t_send,
     grad_t,
@@ -80,8 +83,6 @@
     dx_recv,
     dz_send,
     dz_recv,
-    dl_send,
-    dl_recv,
     cg_vmem,
     dg_vmem,
     last_sum,
@@ -107,6 +108,7 @@
     ys = [(wide_of(y + d, z, xh), n) for d in range(1, NY)]
     zs = [(wide_of(y, z + d, xh), n) for d in range(1, NZ)]
     other_c = n + 1 - 2 * c
+    zs_crossed = [(to, other_c) for to, _ in zs]
     across = wide_of(y, z, 1 - xh)
     other_l = (n + 2) % 4
     beside = wide_of(y, z + 1 - 2 * pair, xh)
@@ -119,7 +121,7 @@
     ]
 
     barrier = pltpu.get_barrier_semaphore()
-    partners = near + depth + ys + zs + [to for dy, dx, dl, to in xys if dy and (dx or dl)]
+    partners = near + depth + ys + zs + zs_crossed + [to for dy, dx, dl, to in xys if dy and (dx or dl)]
     for who in partners:
         pl.semaphore_signal(barrier, inc=1, device_id=who, device_id_type=MESH)
 
@@ -259,6 +261,16 @@
     for s in range(4):
         block = patches[:, 256 * s : 256 * s + 256].astype(F32)
         patches_t[256 * s : 256 * s + 256, :] = block.T.astype(BF)
+
+    row = lax.broadcasted_iota(jnp.int32, (256, 256), 0)
+    column = lax.broadcasted_iota(jnp.int32, (256, 256), 1)
+    q = row % 128
+    source = (q // 32) * 64 + ((q // 4) % 8) * 8 + (1 - row // 128) * 4 + q % 4
+    order[...] = jnp.where(column == source, 1.0, 0.0).astype(BF)
+    row = lax.broadcasted_iota(jnp.int32, (128, 128), 0)
+    column = lax.broadcasted_iota(jnp.int32, (128, 128), 1)
+    source = ((row // 4) % 4) * 32 + (row // 16) * 4 + row % 4
+    order_z[...] = jnp.where(column == source, 1.0, 0.0).astype(BF)
 
     def window(buf, plane, first):
         return [buf[half, plane, first : first + 8].reshape(256, 128) for half in range(2)]
@@ -306,12 +318,7 @@
     for half in range(2):
         grad[half, 1, 1:9] = grad_pre[:, 128 * half : 128 * half + 128].reshape(8, 32, 128)
 
-    row = lax.broadcasted_iota(jnp.int32, (256, 256), 0)
-    column = lax.broadcasted_iota(jnp.int32, (256, 256), 1)
-    q = row % 128
-    source = (q // 32) * 64 + ((q // 4) % 8) * 8 + (1 - row // 128) * 4 + q % 4
-    order = jnp.where(column == source, 1.0, 0.0).astype(BF)
-    turned = matmul_nt(order, grad_pre).astype(BF)
+    turned = matmul_nt(order[...], grad_pre).astype(BF)
     grad_t_send[0] = turned[:128]
     grad_t_send[1] = turned[128:]
     slot = 2 * pair + c
@@ -348,12 +355,8 @@
     for d in Y_ORDER:
         send(CONV_Y, cy_send.at[(y + d) % NY], cy_recv.at[d - 1], ys[d - 1])
     sent(CONV_Y, cy_recv)
-    row = lax.broadcasted_iota(jnp.int32, (128, 128), 0)
-    column = lax.broadcasted_iota(jnp.int32, (128, 128), 1)
-    source = ((row // 4) % 4) * 32 + (row // 16) * 4 + row % 4
-    order = jnp.where(column == source, 1.0, 0.0).astype(BF)
     for k in range(3):
-        grad_rows_z[128 * k : 128 * k + 128, :] = matmul(order, grad_rows[128 * k : 128 * k + 128, :]).astype(BF)
+        grad_rows_z[128 * k : 128 * k + 128, :] = matmul(order_z[...], grad_rows[128 * k : 128 * k + 128, :]).astype(BF)
     slab = jnp.concatenate([cells_at(i, j) for i, j in Z_TAPS], axis=1)
     term = matmul(grad_rows_z[...], slab).astype(BF)
     for zz in range(NZ):
@@ -452,7 +455,9 @@
         total = total + dx_recv[s].astype(F32)
     dz_send[...] = total.reshape(NZ, 8, 128)
     for d in Z_ORDER:
+        send(DOWN_Z, dz_send.at[(z + d) % NZ], dz_recv.at[NZ - 1 + d], zs_crossed[d - 1])
         send(DOWN_Z, dz_send.at[(z + d) % NZ], dz_recv.at[d - 1], zs[d - 1])
+    send(DOWN_Z, dz_send.at[z], dz_recv.at[NZ - 1], (w, other_c))
     sent(DOWN_Z, dz_recv)
 
     arrived(ACT, act_recv.at[pl.ds(0, 3)])
@@ -500,11 +505,15 @@
 
     arrived(DOWN_Z, dz_recv)
     total = dz_send[pl.ds(z, 1)].reshape(8, 128)
-    for d in range(7):
+    for d in range(NZ - 1):
         total = total + dz_recv[d]
-    dl_send[...] = total
-    send(DOWN_LAST, dl_send, dl_recv, (w, other_c))
-    sent(DOWN_LAST, dl_send)
+    theirs = dz_recv[NZ - 1]
+    for d in range(NZ, 2 * NZ - 1):
+        theirs = theirs + dz_recv[d]
+    both = jnp.concatenate([jnp.where(c == 0, total, theirs), jnp.where(c == 0, theirs, total)], axis=1)
+    dg_vmem[...] = jnp.where(c == 0, both[:4], both[4:]) * factor
+    dg_write = pltpu.make_async_copy(dg_vmem, dg_out, local_sem.at[3])
+    dg_write.start()
 
     @pl.when(xh != c)
     def _():
@@ -528,13 +537,6 @@
             cg_vmem[9 * i + 3 * j + m % 3] = conv[4 * (m % 4) : 4 * (m % 4) + 4, at : at + 64]
     cg_write = pltpu.make_async_copy(cg_vmem, cg_out, local_sem.at[2])
     cg_write.start()
-    arrived(DOWN_LAST, dl_recv)
-    theirs = dl_recv[...]
-    both = jnp.concatenate([jnp.where(c == 0, total, theirs), jnp.where(c == 0, theirs, total)], axis=1)
-    dg_vmem[...] = jnp.where(c == 0, both[:4], both[4:]) * factor
-    dg_write = pltpu.make_async_copy(dg_vmem, dg_out, local_sem.at[3])
-    dg_write.start()
-
     flush(range(GROUPS))
     for copy in (vg_write, act_write, cg_write, dg_write):
         copy.wait()
@@ -567,6 +569,8 @@
         ((1024, 256), BF),
         ((2, 3, 10, 32, 128), BF),
         ((2, 3, 10, 32, 128), BF),
+        ((256, 256), BF),
+        ((128, 128), BF),
         ((3, 2, 18, 32, 128), BF),
         ((2, 128, 256), BF),
         ((4, 128, 256), BF),
@@ -595,9 +599,7 @@
         ((2, 2, 16, 16, 128), BF),
         ((15, 4, 16, 128), BF),
         ((8, 8, 128), F32),
-        ((7, 8, 128), F32),
-        ((8, 128), F32),
-        ((8, 128), F32),
+        ((15, 8, 128), F32),
         ((27, 4, 64), F32),
         ((4, 256), F32),
         ((2, 16, 128 * (Y_BLOCKS + Z_BLOCKS)), F32),
@@ -622,7 +624,7 @@
             pltpu.SemaphoreType.DMA((GROUPS,)),
         ],
         compiler_params=pltpu.CompilerParams(
-            collective_id=0, has_side_effects=True, vmem_limit_bytes=56 * 1024 * 1024
+            collective_id=0, has_side_effects=True, vmem_limit_bytes=VMEM_BYTES
         ),
         cost_estimate=pl.CostEstimate(flops=3200000000, bytes_accessed=8000000, transcendentals=65536),
     )(
@@ -638,6 +640,7 @@
         in_specs=[vmem] * 4,
         out_specs=(hbm,) * 4,
         scratch_shapes=[pltpu.SemaphoreType.DMA((4,))],
+        compiler_params=pltpu.CompilerParams(vmem_limit_bytes=VMEM_BYTES),
     )(*results)
     return (
         activated.reshape(1, 32, 32, 64),

time: 49.1 us -> 48.1 us (0.980)
  Pallas kernels: 48.4 us -> 47.4 us
    pallas_call x1, Pallas kernels: 46.4 us -> 45.3 us  [on_device(): pl.pallas_call(functools.partial(kernel, factor), name='unet_level', out_...]
where the time goes in v6:
time: 48.1 us; the launch traced here: 48 us
  Pallas kernels  47.4 us (99%)
  between operations  0.64 us (1%)
    pallas_call x1, Pallas kernels, on_device(): pl.pallas_call(functools.partial(kernel, factor), name='unet_level', out_...  45.3 us
    pallas_call x1, Pallas kernels, on_device(): pl.pallas_call(write_out, name='write_out', out_shape=tuple((jax.ShapeDty...  2.04 us

profile of v6, /device:TPU:1, one launch (start us, length us, event | category | flops | bytes accessed | tf_op | source)
XLA Modules:
  0.0 48.0 jit_solution(4999071355358980623)
XLA Ops:
  0.6 45.3 %unet_level.1 = (bf16[1024,64]{1,0:T(8,128)(2,1)}, bf16[2,8,2,64,128]{4,3,2,1,0:T(8,128)(2,1)}, f32[4,256]{1,0:T(4,128)S(1)}, f32[27,4,64]{2,1,0:T(4,128)S(1)}) custom-call(bf16[2,8,2,64,128]{4,3,2,1,0:T(8,128)(2,1)} %bitcast.5, bf16[1024,256]{1,0:T(8,128)(2,1)} %dw_ref.1, bf16[27,256,256]{2,1,0:T(8,128)(2,1)} %cw_ref.1, bf16[4,256,64]{2,1,0:T(8,128)(2,1)} %bitcast.7), custom_call_target="tpu_custom_call" | custom-call | flops 3200000000 | bytes 8000000 | tf_op jit(solution)/shard_map/unet_level/pallas_call | solution.py:609
  46.0 2.0 %write_out.1 = (bf16[1024,64]{1,0:T(8,128)(2,1)}, bf16[2,8,2,64,128]{4,3,2,1,0:T(8,128)(2,1)}, f32[4,256]{1,0:T(4,128)}, f32[27,4,64]{2,1,0:T(4,128)}) custom-call(bf16[1024,64]{1,0:T(8,128)(2,1)} %get-tuple-element.12.refs_0_, bf16[2,8,2,64,128]{4,3,2,1,0:T(8,128)(2,1)} %get-tuple-element.13.refs_1_, f32[4,256]{1,0:T(4,128)S(1)} %get-tuple-element.14.refs_2_, ...), custom_call_target="tpu_custom_call" | custom-call | tf_op jit(solution)/shard_map/write_out/pallas_call | solution.py:636

commit v7 on v6

--- a/solution.py
+++ b/solution.py
@@ -9,7 +9,7 @@
 from jax.sharding import PartitionSpec as P
 
 MESH = pl.DeviceIdType.MESH
-VMEM_BYTES = 55040 * 1024
+VMEM_BYTES = 54784 * 1024
 BF = jnp.bfloat16
 F32 = jnp.float32
 Y_TAPS = ((0, 0), (0, 1), (0, 2), (1, 0), (1, 1), (1, 2))
@@ -114,11 +114,17 @@
     beside = wide_of(y, z + 1 - 2 * pair, xh)
     xys = [
         (dy, dx, dl, (wide_of(y + dy, z, (xh + dx) % 2), n + 2 * dl * (1 - 2 * l)))
-        for dy in range(NY)
-        for dx in range(2)
-        for dl in range(2)
+        for dy in (2, 1, 3, 0)
+        for dx, dl in ((1, 0), (0, 1), (1, 1), (0, 0))
         if dy or dx or dl
     ]
+
+    loads = [
+        pltpu.make_async_copy(src, dst, local_sem.at[s])
+        for s, (src, dst) in enumerate(((vol_ref, vol), (dw_ref, dw), (cot_ref, cot), (cw_ref, cw)))
+    ]
+    for copy in loads[:3]:
+        copy.start()
 
     barrier = pltpu.get_barrier_semaphore()
     partners = near + depth + ys + zs + zs_crossed + [to for dy, dx, dl, to in xys if dy and (dx or dl)]
@@ -165,12 +171,6 @@
             finish(*group, False)
             outgoing.remove(group)
 
-    loads = [
-        pltpu.make_async_copy(src, dst, local_sem.at[s])
-        for s, (src, dst) in enumerate(((vol_ref, vol), (dw_ref, dw), (cot_ref, cot), (cw_ref, cw)))
-    ]
-    for copy in loads:
-        copy.start()
 
     inside = (n == 1) | (n == 2)
     far = (w + 63 + 2 * xh) % 64
@@ -223,6 +223,7 @@
                 at = (4 * a + 2 * b + e) * 128
                 patches[:, at : at + 128] = part
     loads[1].wait()
+    loads[3].start()
     cells = matmul(patches[...], dw[...]).astype(BF)
     for half in range(2):
         deep[half, 1, 1:9] = cells[:, 128 * half : 128 * half + 128].reshape(8, 32, 128)
@@ -246,13 +247,13 @@
         arrived(received, theirs)
         to_core(theirs, plane, 1 - pair)
 
-    pl.semaphore_wait(barrier, len(partners))
-    send_halos(deep, DEEP_ROWS)
     loads[2].wait()
     for m in range(4):
         cot_send[m] = jnp.concatenate([cot[m, :128], cot[m, 128:]], axis=1)
     cot_recv[pl.ds(n, 1)] = cot_send[pl.ds(n, 1)]
-    for d in range(1, 4):
+    pl.semaphore_wait(barrier, len(partners))
+    send_halos(deep, DEEP_ROWS)
+    for d in (1, 3, 2):
         send(COT, cot_send.at[(n + d) % 4], cot_recv.at[n], near[d - 1])
     sent(COT, cot_send.at[pl.ds(0, 3)])
     cyz_rows[...] = jnp.zeros_like(cyz_rows)
@@ -394,7 +395,7 @@
         part = activated[:, 64 * m : 64 * m + 64]
         act_send[m] = jnp.concatenate([part[:128], part[128:]], axis=1)
     act_recv[pl.ds(n, 1)] = act_send[pl.ds(n, 1)]
-    for d in range(1, 4):
+    for d in (1, 3, 2):
         send(ACT, act_send.at[(n + d) % 4], act_recv.at[n], near[d - 1])
     sent(ACT, act_send.at[pl.ds(0, 3)])
 

time: 48.1 us -> 48 us (level)
  no operation moved by 1% of the time
where the time goes in v7:
time: 48 us; the launch traced here: 47.8 us
  Pallas kernels  47.1 us (98%)
  between operations  0.64 us (1%)
    pallas_call x1, Pallas kernels, on_device(): pl.pallas_call(functools.partial(kernel, factor), name='unet_level', out_...  45.2 us
    pallas_call x1, Pallas kernels, on_device(): pl.pallas_call(write_out, name='write_out', out_shape=tuple((jax.ShapeDty...  1.96 us

profile of v7, /device:TPU:1, one launch (start us, length us, event | category | flops | bytes accessed | tf_op | source)
XLA Modules:
  0.0 47.8 jit_solution(8709556243333252400)
XLA Ops:
  0.6 45.2 %unet_level.1 = (bf16[1024,64]{1,0:T(8,128)(2,1)S(1)}, bf16[2,8,2,64,128]{4,3,2,1,0:T(8,128)(2,1)}, f32[4,256]{1,0:T(4,128)S(1)}, f32[27,4,64]{2,1,0:T(4,128)S(1)}) custom-call(bf16[2,8,2,64,128]{4,3,2,1,0:T(8,128)(2,1)} %bitcast.5, bf16[1024,256]{1,0:T(8,128)(2,1)} %dw_ref.1, bf16[27,256,256]{2,1,0:T(8,128)(2,1)} %cw_ref.1, bf16[4,256,64]{2,1,0:T(8,128)(2,1)} %bitcast.7), custom_call_target="tpu_custom_call" | custom-call | flops 3200000000 | bytes 8000000 | tf_op jit(solution)/shard_map/unet_level/pallas_call | solution.py:610
  45.8 2.0 %write_out.1 = (bf16[1024,64]{1,0:T(8,128)(2,1)}, bf16[2,8,2,64,128]{4,3,2,1,0:T(8,128)(2,1)}, f32[4,256]{1,0:T(4,128)}, f32[27,4,64]{2,1,0:T(4,128)}) custom-call(bf16[1024,64]{1,0:T(8,128)(2,1)S(1)} %get-tuple-element.12.refs_0_, bf16[2,8,2,64,128]{4,3,2,1,0:T(8,128)(2,1)} %get-tuple-element.13.refs_1_, f32[4,256]{1,0:T(4,128)S(1)} %get-tuple-element.14.refs_2_, ...), custom_call_target="tpu_custom_call" | custom-call | tf_op jit(solution)/shard_map/write_out/pallas_call | solution.py:637

commit v8 on v7

--- a/solution.py
+++ b/solution.py
@@ -347,14 +347,18 @@
         return jnp.concatenate([deep_all[i, s, j : j + 16].reshape(512, 128) for s in range(2)], axis=0)
 
     arrived(DEEP_CORE, deep_all.at[:, :, pl.ds(0, 9)])
-    slab = jnp.concatenate([cells_at(i, j) for i, j in Y_TAPS], axis=1)
-    term = matmul(grad_rows[...], slab).astype(BF)
-    for yy in range(NY):
-        for k in range(3):
-            at = 128 * k + 32 * yy
-            cy_send[yy, k] = term[at : at + 32]
-    for d in Y_ORDER:
-        send(CONV_Y, cy_send.at[(y + d) % NY], cy_recv.at[d - 1], ys[d - 1])
+    for first in (0, YL // 2):
+        lanes = pl.ds(first, YL // 2)
+        some = Y_TAPS[first // 128 : (first + YL // 2) // 128]
+        slab = jnp.concatenate([cells_at(i, j) for i, j in some], axis=1)
+        term = matmul(grad_rows[...], slab).astype(BF)
+        for yy in range(NY):
+            for k in range(3):
+                at = 128 * k + 32 * yy
+                cy_send[yy, k, :, first : first + YL // 2] = term[at : at + 32]
+        for d in Y_ORDER:
+            src = cy_send.at[(y + d) % NY, :, :, lanes]
+            send(CONV_Y, src, cy_recv.at[d - 1, :, :, lanes], ys[d - 1])
     sent(CONV_Y, cy_recv)
     for k in range(3):
         grad_rows_z[128 * k : 128 * k + 128, :] = matmul(order_z[...], grad_rows[128 * k : 128 * k + 128, :]).astype(BF)

time: 48 us -> 47.2 us (0.983)
  Pallas kernels: 47.1 us -> 46.3 us
    pallas_call x1, Pallas kernels: 45.2 us -> 44.4 us  [on_device(): pl.pallas_call(functools.partial(kernel, factor), name='unet_level', out_...]
where the time goes in v8:
time: 47.2 us; the launch traced here: 47 us
  Pallas kernels  46.3 us (98%)
  between operations  0.64 us (1%)
    pallas_call x1, Pallas kernels, on_device(): pl.pallas_call(functools.partial(kernel, factor), name='unet_level', out_...  44.4 us
    pallas_call x1, Pallas kernels, on_device(): pl.pallas_call(write_out, name='write_out', out_shape=tuple((jax.ShapeDty...  1.96 us

profile of v8, /device:TPU:1, one launch (start us, length us, event | category | flops | bytes accessed | tf_op | source)
XLA Modules:
  0.0 47.0 jit_solution(1494373247374301650)
XLA Ops:
  0.6 44.4 %unet_level.1 = (bf16[1024,64]{1,0:T(8,128)(2,1)S(1)}, bf16[2,8,2,64,128]{4,3,2,1,0:T(8,128)(2,1)}, f32[4,256]{1,0:T(4,128)S(1)}, f32[27,4,64]{2,1,0:T(4,128)S(1)}) custom-call(bf16[2,8,2,64,128]{4,3,2,1,0:T(8,128)(2,1)} %bitcast.5, bf16[1024,256]{1,0:T(8,128)(2,1)} %dw_ref.1, bf16[27,256,256]{2,1,0:T(8,128)(2,1)} %cw_ref.1, bf16[4,256,64]{2,1,0:T(8,128)(2,1)} %bitcast.7), custom_call_target="tpu_custom_call" | custom-call | flops 3200000000 | bytes 8000000 | tf_op jit(solution)/shard_map/unet_level/pallas_call | solution.py:614
  45.0 2.0 %write_out.1 = (bf16[1024,64]{1,0:T(8,128)(2,1)}, bf16[2,8,2,64,128]{4,3,2,1,0:T(8,128)(2,1)}, f32[4,256]{1,0:T(4,128)}, f32[27,4,64]{2,1,0:T(4,128)}) custom-call(bf16[1024,64]{1,0:T(8,128)(2,1)S(1)} %get-tuple-element.12.refs_0_, bf16[2,8,2,64,128]{4,3,2,1,0:T(8,128)(2,1)} %get-tuple-element.13.refs_1_, f32[4,256]{1,0:T(4,128)S(1)} %get-tuple-element.14.refs_2_, ...), custom_call_target="tpu_custom_call" | custom-call | tf_op jit(solution)/shard_map/write_out/pallas_call | solution.py:641
